TPU v7x, 256 devices: a whole 4x4x8 slice. The times are simulated.
256 devices in a mesh: dp: 4 (over y_hi, core), context: 16 (over y_lo, z), tensor: 4 (over x).
Axes of the slice: x: 4, y: 4 (y_hi: 2, y_lo: 2; y = y_hi * 2 + y_lo), z: 8, core: 2. Of those that a mesh axis runs over, the one named last changes fastest.
Arguments:
- queries: bfloat16 [8192, 4608], P(('dp', 'context'), 'tensor'), may hold values from -6 to 6
- keys: bfloat16 [8192, 4608], P(('dp', 'context'), 'tensor'), may hold values from -6 to 6
- values: bfloat16 [8192, 4608], P(('dp', 'context'), 'tensor'), may hold values from -7.5 to 7.5
- residual: bfloat16 [8192, 4608], P(('dp', 'context'), 'tensor'), may hold values from -120 to 120
- norm_gain: float32 [4608], P('tensor'), may hold values from 0.1 to 1.9
- routes: int32 [8192, 2], P(('dp', 'context')), may hold values from 0 to 15, all different within a row; in each aligned block of 128 rows (0 to 127, 128 to 255, ...) at most 17 rows name the same one
- route_weight: float32 [8192, 2], P(('dp', 'context')), may hold values from 0.2 to 1
- w_gate: bfloat16 [16, 4608, 6144], P(('dp', 'tensor'), None, 'context'), may hold values from -0.09375 to 0.09375
- w_up: bfloat16 [16, 4608, 6144], P(('dp', 'tensor'), None, 'context'), may hold values from -0.09375 to 0.09375
- w_down: bfloat16 [16, 6144, 4608], P(('dp', 'tensor'), 'context'), may hold values from -0.078125 to 0.078125
- scale_hidden: float32 [16, 2, 6144], P(('dp', 'tensor'), None, 'context'), may hold values from 0.5 to 2
- scale_out: float32 [16, 4608], P(('dp', 'tensor')), may hold values from 0.5 to 2
Outputs:
- output: bfloat16 [8192, 4608], P(('dp', 'context'), 'tensor')
Inputs may be any that keep to these rules, and one draw needn't show every extreme that they name: In each aligned block of 128 tokens no expert is named by more than 17 of the block's routes, a bound that some block reaches. Every expert is named somewhere.
All inputs are finite; a program needn't handle non-finite values.
Results may differ from a plain program's by a relative error of at most 0.0095.
Values may be sent and summed in bfloat16 or wider, within the bound.
A program may use at most 128 MiB of HBM per device.

v0:
```python
import math

import jax
import jax.numpy as jnp
from jax import lax
from jax.sharding import PartitionSpec as P

D = 4608
HD = 128
EXPERTS = 16
TOP = 2
CAP = 17


EPS = 1e-06
NEG = -1e30


def activate(rows_in, gate_mat, up_mat, gate_scale, up_scale):
    gate_val = jnp.dot(rows_in, gate_mat, preferred_element_type=jnp.float32) * gate_scale
    up_val = jnp.dot(rows_in, up_mat, preferred_element_type=jnp.float32) * up_scale
    return (jax.nn.silu(gate_val) * up_val).astype(jnp.bfloat16)


def local(
    queries,
    keys,
    values,
    residual,
    norm_gain,
    routes,
    route_weight,
    w_gate,
    w_up,
    w_down,
    scale_hidden,
    scale_out,
):
    tok_rows = queries.shape[0]
    quarter = queries.shape[1]
    heads_here = quarter // HD
    n_dp = lax.axis_size("dp")
    n_tensor = lax.axis_size("tensor")
    inv_root = 1.0 / math.sqrt(HD)
    query_heads = queries.reshape(tok_rows, heads_here, HD)
    query_pos = lax.axis_index("context") * tok_rows + jnp.arange(tok_rows, dtype=jnp.int32)
    running_max = jnp.full((heads_here, tok_rows), NEG, jnp.float32)
    key_shard = lax.all_gather(keys, "context", axis=0, tiled=True)
    value_shard = lax.all_gather(values, "context", axis=0, tiled=True)
    length = key_shard.shape[0]
    key_heads = key_shard.reshape(length, heads_here, HD)
    value_heads = value_shard.reshape(length, heads_here, HD)
    scores = (
        jnp.einsum("qhd,khd->hqk", query_heads, key_heads, preferred_element_type=jnp.float32)
        * inv_root
    )
    key_pos = jnp.arange(length, dtype=jnp.int32)
    allowed = (query_pos[:, None] >= key_pos[None, :])[None]
    new_max = jnp.maximum(running_max, jnp.max(jnp.where(allowed, scores, NEG), axis=2))
    weights = jnp.where(allowed, jnp.exp(scores - new_max[:, :, None]), 0.0)
    new_sum = jnp.sum(weights, axis=2)
    contrib = jnp.einsum(
        "hqk,khd->hqd",
        weights.astype(jnp.bfloat16),
        value_heads,
        preferred_element_type=jnp.float32,
    )
    attended = (
        (contrib / new_sum[:, :, None])
        .transpose(1, 0, 2)
        .reshape(tok_rows, quarter)
        .astype(jnp.bfloat16)
    )
    hidden_state = residual.astype(jnp.float32) + lax.optimization_barrier(attended).astype(
        jnp.float32
    )
    square_total = lax.psum(jnp.sum(hidden_state * hidden_state, axis=1), "tensor")
    inverse = lax.rsqrt(square_total / D + EPS)
    normed = (hidden_state * inverse[:, None] * norm_gain[None, :]).astype(jnp.bfloat16)
    flat_routes = routes.reshape(-1)
    route_rows = flat_routes.shape[0]
    member = (flat_routes[:, None] == jnp.arange(EXPERTS, dtype=jnp.int32)[None, :]).astype(
        jnp.int32
    )
    ranks = jnp.sum((jnp.cumsum(member, axis=0) - member) * member, axis=1)
    slot_index = flat_routes * CAP + ranks
    slot_hit = (slot_index[:, None] == jnp.arange(EXPERTS * CAP, dtype=jnp.int32)[None, :]).astype(
        jnp.float32
    )
    token_hit = (
        (jnp.arange(route_rows, dtype=jnp.int32) // TOP)[:, None]
        == jnp.arange(tok_rows, dtype=jnp.int32)[None, :]
    ).astype(jnp.float32)
    dispatch = jnp.dot(slot_hit.T, token_hit, precision=lax.Precision.HIGHEST).astype(jnp.bfloat16)
    combine = jnp.dot(
        token_hit.T, slot_hit * route_weight.reshape(-1)[:, None], precision=lax.Precision.HIGHEST
    )
    tensor_pos = lax.axis_index("tensor")
    widened = lax.all_gather(normed, "tensor", axis=1, tiled=True)
    own_slots = lax.dynamic_index_in_dim(
        dispatch.reshape(n_dp, n_tensor, CAP, tok_rows), tensor_pos, axis=1, keepdims=False
    ).reshape(n_dp * CAP, tok_rows)
    outgoing = jnp.dot(own_slots, widened, preferred_element_type=jnp.float32).astype(jnp.bfloat16)
    expert_rows = lax.all_to_all(outgoing, "dp", split_axis=0, concat_axis=0, tiled=True)
    activated = activate(
        lax.all_gather(expert_rows, "context", axis=0, tiled=True),
        w_gate[0],
        w_up[0],
        scale_hidden[0, 0][None, :],
        scale_hidden[0, 1][None, :],
    )
    summed = lax.psum_scatter(
        jnp.dot(activated, w_down[0], preferred_element_type=jnp.float32).astype(jnp.bfloat16),
        "context",
        scatter_dimension=0,
        tiled=True,
    ).astype(jnp.float32)
    expert_out = (summed * scale_out[0][None, :]).astype(jnp.bfloat16)
    returned = lax.all_to_all(expert_out, "dp", split_axis=0, concat_axis=0, tiled=True)
    own_combine = lax.dynamic_index_in_dim(
        combine.reshape(tok_rows, n_dp, n_tensor, CAP), tensor_pos, axis=2, keepdims=False
    ).reshape(tok_rows, n_dp * CAP)
    partial_full = jnp.dot(
        own_combine, returned.astype(jnp.float32), precision=lax.Precision.HIGHEST
    )
    routed = lax.psum_scatter(
        partial_full.astype(jnp.bfloat16), "tensor", scatter_dimension=1, tiled=True
    ).astype(jnp.float32)
    return (hidden_state + routed).astype(jnp.bfloat16)


def solution(mesh):
    in_specs = (
        P(("dp", "context"), "tensor"),
        P(("dp", "context"), "tensor"),
        P(("dp", "context"), "tensor"),
        P(("dp", "context"), "tensor"),
        P("tensor"),
        P(("dp", "context"), None),
        P(("dp", "context"), None),
        P(("dp", "tensor"), None, "context"),
        P(("dp", "tensor"), None, "context"),
        P(("dp", "tensor"), "context", None),
        P(("dp", "tensor"), None, "context"),
        P(("dp", "tensor"), None),
    )
    out_specs = P(("dp", "context"), "tensor")
    return jax.shard_map(local, mesh=mesh, in_specs=in_specs, out_specs=out_specs, check_vma=False)
```

profile of v0, /device:TPU:8, one launch (start us, length us, event | category | flops | bytes accessed | tf_op | source)
XLA Modules:
  0.0 638.6 jit_solution(12395793537640012072)
XLA Ops:
  12.1 93.4 %all-gather.6.cloned.1.call-done = bf16[2048,1152]{0,1:T(8,128)(2,1)} async-done(((bf16[128,1152]{0,1:T(8,128)(2,1)}), bf16[2048,1152]{0,1:T(8,128)(2,1)}) %all-gather.6.cloned.1.call-update) | async-done | bytes 4718608 | tf_op jit(solution)/shard_map/all_gather | solution.py:48
  105.6 4.7 select_reduce_fusion
  110.3 3.6 copy-done.1
  113.9 2.9 fusion.1
  116.8 67.0 %all-gather.8.cloned.1.call-done = bf16[2048,1152]{1,0:T(8,128)(2,1)} async-done(((bf16[128,1152]{1,0:T(8,128)(2,1)}), bf16[2048,1152]{1,0:T(8,128)(2,1)}) %all-gather.8.cloned.1.call-update) | async-done | bytes 4718608 | tf_op jit(solution)/shard_map/all_gather | solution.py:49
  183.8 6.7 %copy.30 = bf16[2048,1152]{0,1:T(8,128)(2,1)} copy(bf16[2048,1152]{1,0:T(8,128)(2,1)} %all-gather.8.cloned.1.call-done) | data formatting | bytes 9437184 | tf_op jit(solution)/shard_map/all_gather | solution.py:49
  190.5 8.1 %fusion.39 = bf16[128,9,128]{0,2,1:T(8,128)(2,1)} fusion(bf16[2048,9,128]{0,2,1:T(8,128)(2,1)} %bitcast.68, f32[9,128,2048]{2,1,0:T(8,128)} %copy-done.1, f32[9,128]{1,0:T(8,128)S(1)} %broadcast_maximum_fusion, pred[128,2048]{1,0:T(8,128)(4,1)} %iota_compare_fusion, f32[128,9]{0,1:T(8,128)} %bitcast.73), kind=kOutput, calls=%fused_computation.31 | convolution fusion | flops 613711872 | bytes 14722048 | tf_op jit(solution)/shard_map/hqk,khd->hqd/dot_general | solution.py:62
  201.7 10.5 %psum.7 = f32[128]{0:T(128)S(1)} all-reduce(f32[128]{0:T(128)S(1)} %multiply_reduce_fusion), channel_id=1, replica_groups=mesh['dp'=4,'context'=16,'tensor'=4] {'tensor'}, use_global_device_ids=true, to_apply=%region_6.7 | all-reduce | flops 128 | bytes 1024 | tf_op jit(solution)/shard_map/psum | solution.py:77
  229.8 7.7 %all-gather.10.cloned.1.call-done = bf16[128,4608]{1,0:T(8,128)(2,1)} async-done(((bf16[128,1152]{1,0:T(8,128)(2,1)}), bf16[128,4608]{1,0:T(8,128)(2,1)}) %all-gather.10.cloned.1.call-update) | async-done | bytes 1179664 | tf_op jit(solution)/shard_map/all_gather | solution.py:99
  237.6 2.5 convolution_convert_fusion.2
  242.2 18.5 %all_to_all.24 = bf16[4,17,4608]{2,1,0:T(8,128)(2,1)} all-to-all(bf16[4,17,4608]{2,1,0:T(8,128)(2,1)} %all_to_all.16), channel_id=1, replica_groups=mesh['dp'=4,'context'=16,'tensor'=4] {'dp'}, dimensions={0} | all-to-all | bytes 1253376 | tf_op jit(solution)/shard_map/all_to_all | solution.py:104
  263.0 121.5 %all-gather.12.cloned.1.call-done = bf16[16,68,4608]{2,1,0:T(8,128)(2,1)} async-done(((bf16[1,68,4608]{2,1,0:T(8,128)(2,1)}), bf16[16,68,4608]{2,1,0:T(8,128)(2,1)}) %all-gather.12.cloned.1.call-update) | async-done | bytes 10027024 | tf_op jit(solution)/shard_map/all_gather | solution.py:106
  384.6 10.7 %reshape.112 = bf16[1088,4608]{1,0:T(8,128)(2,1)} reshape(bf16[16,68,4608]{2,1,0:T(8,128)(2,1)} %all-gather.12.cloned.1.call-done) | data formatting | bytes 20054016
  395.2 9.9 %fusion.14 = f32[1088,384]{1,0:T(8,128)} fusion(bf16[1088,4608]{1,0:T(8,128)(2,1)} %reshape.112, bf16[1,4608,384]{2,1,0:T(8,128)(2,1)} %param.19, f32[384]{0:T(512)S(1)} %get-tuple-element.6), kind=kOutput, calls=%fused_computation.17 | convolution fusion | flops 3850788864 | bytes 15238656 | tf_op jit(solution)/shard_map/dot_general | solution.py:20
  405.2 16.8 %convolution_convert_fusion = bf16[1088,4608]{1,0:T(8,128)(2,1)} fusion(bf16[1,384,4608]{2,1,0:T(8,128)(2,1)S(1)} %copy-done, bf16[1088,4608]{1,0:T(8,128)(2,1)} %reshape.112, bf16[1,4608,384]{2,1,0:T(8,128)(2,1)} %param.20, f32[1088,384]{1,0:T(8,128)} %fusion.14, f32[384]{0:T(512)S(1)} %get-tuple-element.5), kind=kOutput, calls=%fused_computation | convolution fusion | flops 7708680192 | bytes 28804608 | tf_op jit(solution)/shard_map/dot_general | solution.py:113
  421.9 122.8 %fusion = bf16[72,4608]{1,0:T(8,128)(2,1)} fusion(bf16[1088,4608]{1,0:T(8,128)(2,1)} %convolution_convert_fusion), kind=kCustom, calls=%all-reduce-scatter | all-reduce-scatter fusion | flops 5308417 | bytes 10691584
  546.7 2.4 collective-permute-start
  551.8 13.1 %collective-permute-done = bf16[60,4608]{1,0:T(8,128)(2,1)} collective-permute-done((bf16[60,4608]{1,0:T(8,128)(2,1)}, bf16[60,4608]{1,0:T(8,128)(2,1)}, u32[]{:S(2)}, u32[]{:S(2)}) %collective-permute-start) | collective-permute-done | bytes 552992
  564.9 10.2 %concatenate = bf16[132,4608]{1,0:T(8,128)(2,1)} concatenate(bf16[60,4608]{1,0:T(8,128)(2,1)} %collective-permute-done, bf16[72,4608]{1,0:T(8,128)(2,1)} %fusion), dimensions={0} | concatenate | bytes 2433024
  579.6 4.2 all-to-all-start.1
  591.3 6.8 %all-to-all-done.1 = bf16[4,17,4608]{2,1,0:T(8,128)(2,1)} async-done(((bf16[4,17,4608]{2,1,0:T(8,128)(2,1)}), bf16[4,17,4608]{2,1,0:T(8,128)(2,1)}, u32[]{:S(2)}, u32[]{:S(2)}) %all-to-all-start.1) | async-done | bytes 626720 | tf_op jit(solution)/shard_map/all_to_all | solution.py:119
  600.3 3.3 convolution_convert_fusion.1
  603.6 2.4 copy.38
  606.0 22.3 %reduce-scatter.6.cloned.1.call-done = bf16[1152,128]{1,0:T(8,128)(2,1)} async-done(((bf16[4608,128]{1,0:T(8,128)(2,1)}), bf16[1152,128]{1,0:T(8,128)(2,1)}) %reduce-scatter.6.cloned.1.call-update) | async-done | bytes 294928
  (67 shorter events, 52.8 us)
Async XLA Ops:
  6.5 398.6 %copy-start = (bf16[1,384,4608]{2,1,0:T(8,128)(2,1)S(1)}, bf16[1,384,4608]{2,1,0:T(8,128)(2,1)}, u32[]{:S(2)}) copy-start(bf16[1,384,4608]{2,1,0:T(8,128)(2,1)} %param.21) | copy-start | bytes 10616836
  6.5 99.0 %all-gather.6.cloned.1.call-start = ((), (), s32[]{:S(2)}) async-start(), calls=%async_computation.3 | async-start | bytes 5013504 | tf_op jit(solution)/shard_map/all_gather | solution.py:48
  8.6 175.2 %all-gather.8.cloned.1.call-start = ((), (), s32[]{:S(2)}) async-start(), calls=%async_computation.4 | async-start | bytes 5013504 | tf_op jit(solution)/shard_map/all_gather | solution.py:49
  9.3 228.2 %all-gather.10.cloned.1.call-start = ((), (), s32[]{:S(2)}) async-start(), calls=%async_computation.5 | async-start | bytes 1474560 | tf_op jit(solution)/shard_map/all_gather | solution.py:99
  105.6 8.4 %copy-start.2 = (pred[128,2048]{1,0:T(8,128)(4,1)S(1)}, pred[128,2048]{1,0:T(8,128)(4,1)}, u32[]{:S(2)}) copy-start(pred[128,2048]{1,0:T(8,128)(4,1)} %iota_compare_fusion) | copy-start | bytes 786436
  110.3 3.6 copy-start.1
  190.5 21.7 %copy-start.3 = (f32[1152]{0:T(1024)S(1)}, f32[1152]{0:T(1024)}, u32[]{:S(2)}) copy-start(f32[1152]{0:T(1024)} %param.16) | copy-start | bytes 13828
  214.1 170.5 %all-gather.12.cloned.1.call-start = ((), (), s32[]{:S(2)}) async-start(), calls=%async_computation.6 | async-start | bytes 11280384 | tf_op jit(solution)/shard_map/all_gather | solution.py:106
  223.4 39.6 %copy-start.4 = (f32[1,2,384]{2,1,0:T(2,128)S(1)}, f32[1,2,384]{2,1,0:T(2,128)}, u32[]{:S(2)}) copy-start(f32[1,2,384]{2,1,0:T(2,128)} %param.22) | copy-start | bytes 9220
  224.1 0.6 copy-start.6
  421.9 128.6 %copy-start.8 = (u32[256]{0:T(256)S(1)}, u32[256]{0:T(256)}, u32[]{:S(2)}) copy-start(u32[256]{0:T(256)} %constant.68) | copy-start | bytes 3076
  544.7 39.2 %copy-start.5 = (f32[128,2]{0,1:T(2,128)S(1)}, f32[128,2]{0,1:T(2,128)}, u32[]{:S(2)}) copy-start(f32[128,2]{0,1:T(2,128)} %param.18) | copy-start | bytes 3076
  544.7 40.9 %copy-start.7 = (s32[256]{0:T(256)S(1)}, s32[256]{0:T(256)}, u32[]{:S(2)}) copy-start(s32[256]{0:T(256)} %copy-done.6) | copy-start | bytes 3076
  546.7 18.2 %collective-permute-start = (bf16[60,4608]{1,0:T(8,128)(2,1)}, bf16[60,4608]{1,0:T(8,128)(2,1)}, u32[]{:S(2)}, u32[]{:S(2)}) collective-permute-start(bf16[60,4608]{1,0:T(8,128)(2,1)} %slice.17), channel_id=1, source_target_pairs={{0,4},{4,8},{8,12},{12,16},{16,20},{20,24},{24,28},{28,32},{32,36}... | collective-permute-start | bytes 1658888
  579.6 18.5 %all-to-all-start.1 = ((bf16[4,17,4608]{2,1,0:T(8,128)(2,1)}), bf16[4,17,4608]{2,1,0:T(8,128)(2,1)}, u32[]{:S(2)}, u32[]{:S(2)}) async-start(bf16[4,17,4608]{2,1,0:T(8,128)(2,1)} %all_to_all.19), calls=%async_computation.1 | async-start | bytes 1769472 | tf_op jit(solution)/shard_map/all_to_all | solution.py:119
  583.8 44.5 %reduce-scatter.6.cloned.1.call-start = ((), (), s32[]{:S(2)}) async-start(), calls=%async_computation.7 | async-start | bytes 1474560
Sparse Core Ops, SparseCore 0:
  9.1 96.4 all-gather.5
  107.4 76.3 all-gather.7
  214.2 23.3 all-gather.9
  263.1 121.3 all-gather.11
  606.1 22.1 reduce-scatter.5
where the time goes:
time: 641 us; the launch traced here: 639 us
  waiting for transfers between devices  333 us (52%)
  blocking collectives  152 us (24%)
  local copies, waits for them, and re-layouts  69.1 us (11%)
  matrix products  47.5 us (7%)
  other arithmetic  17 us (3%)
  between operations  13.9 us (2%)
  starting transfers between devices  6.79 us (1%)
    unnamed x1, blocking collectives  123 us
    all_gather x1, waiting for transfers between devices, local(): lax.all_gather(expert_rows, 'context', axis=0, tiled=True)  122 us
    all_gather x1, waiting for transfers between devices, local(): key_shard = lax.all_gather(keys, 'context', axis=0, tiled=True)  93.4 us
    all_gather x1, waiting for transfers between devices, local(): value_shard = lax.all_gather(values, 'context', axis=0, tiled=True)  67 us
    unnamed x29, local copies, waits for them, and re-layouts  40.2 us
    unnamed x7, waiting for transfers between devices  36.2 us
    all_to_all x1, blocking collectives, local(): lax.all_to_all(outgoing, 'dp', split_axis=0, concat_axis=0, tiled=True)  18.5 us
    dot_general x1, matrix products, local(): jnp.dot(activated, w_down[0], preferred_element_type=jnp.float32)  16.8 us
  transfers between devices with their start and end apart: 7, of which 7 were waited for; matrix products, arithmetic and copies ran while one was open for 5% of the time, Pallas kernels for 0%

commit v1 on v0

--- a/solution.py
+++ b/solution.py
@@ -3,6 +3,8 @@
 import jax
 import jax.numpy as jnp
 from jax import lax
+from jax.experimental import pallas as pl
+from jax.experimental.pallas import tpu as pltpu
 from jax.sharding import PartitionSpec as P
 
 D = 4608
@@ -14,6 +16,176 @@
 
 EPS = 1e-06
 NEG = -1e30
+
+
+N_CTX = 16
+HEADS_HERE = 9
+MESH = pl.DeviceIdType.MESH
+EXP_SCALE = math.log2(math.e) / math.sqrt(HD)
+
+
+def head_owner(head, core):
+    return lax.rem(lax.div(head * N_CTX, HEADS_HERE) + 8 * core, N_CTX)
+
+
+def attention_kernel(
+    q_ref, k_ref, v_ref, out_ref, qs, ks, vs, ob, recv_sem, send_sem, out_send, out_recv
+):
+    ctx = lax.axis_index("context")
+    core = lax.rem(lax.axis_index("dp"), 2)
+    rows = q_ref.shape[0]
+
+    barrier = pltpu.get_barrier_semaphore()
+
+    @pl.loop(1, N_CTX)
+    def _(step):
+        pl.semaphore_signal(
+            barrier, inc=1, device_id={"context": lax.rem(ctx + step, N_CTX)}, device_id_type=MESH
+        )
+
+    pl.semaphore_wait(barrier, N_CTX - 1)
+
+    my_rows = pl.ds(pl.multiple_of(ctx * rows, rows), rows)
+    sources = (k_ref, q_ref, v_ref)
+    targets = (ks, qs, vs)
+
+    def scatter(step, start):
+        head = lax.rem(ctx + step, HEADS_HERE)
+        owner = head_owner(head, core)
+        columns = pl.ds(pl.multiple_of(head * HD, HD), HD)
+        for index in range(3):
+            src = sources[index].at[:, columns]
+            dst = targets[index].at[my_rows, :]
+
+            @pl.when(owner != ctx)
+            def _():
+                copy = pltpu.make_async_remote_copy(
+                    src_ref=src,
+                    dst_ref=dst,
+                    send_sem=send_sem.at[step, index],
+                    recv_sem=recv_sem.at[index],
+                    device_id={"context": owner},
+                    device_id_type=MESH,
+                )
+                if start:
+                    copy.start()
+                else:
+                    copy.wait_send()
+
+            if start:
+
+                @pl.when(owner == ctx)
+                def _():
+                    pltpu.make_async_copy(src, dst, recv_sem.at[index]).start()
+
+    @pl.loop(0, HEADS_HERE)
+    def _(step):
+        scatter(step, True)
+
+    base = lax.rem(ctx + 8 * core, N_CTX)
+    my_head = lax.div(base * HEADS_HERE + N_CTX - 1, N_CTX)
+    active = jnp.logical_and(
+        my_head < HEADS_HERE, lax.div(my_head * N_CTX, HEADS_HERE) == base
+    )
+    head_columns = pl.ds(pl.multiple_of(lax.rem(my_head, HEADS_HERE) * HD, HD), HD)
+
+    def give(block, start):
+        src = ob.at[pl.ds(block * rows, rows), :]
+        dst = out_ref.at[:, head_columns]
+
+        @pl.when(ctx != block)
+        def _():
+            copy = pltpu.make_async_remote_copy(
+                src_ref=src,
+                dst_ref=dst,
+                send_sem=out_send.at[block],
+                recv_sem=out_recv,
+                device_id={"context": block},
+                device_id_type=MESH,
+            )
+            if start:
+                copy.start()
+            else:
+                copy.wait_send()
+
+        if start:
+
+            @pl.when(ctx == block)
+            def _():
+                pltpu.make_async_copy(src, dst, out_recv).start()
+
+    @pl.when(active)
+    def _():
+        for index in range(3):
+            pltpu.make_async_copy(targets[index], targets[index], recv_sem.at[index]).wait()
+        tile = 2 * rows
+        contract = (((1,), (1,)), ((), ()))
+        causal = lax.broadcasted_iota(jnp.int32, (tile, tile), 0) >= lax.broadcasted_iota(
+            jnp.int32, (tile, tile), 1
+        )
+        for number in range(N_CTX // 2 - 1, -1, -1):
+            low, high = number * tile, (number + 1) * tile
+            query = qs[low:high, :]
+            own = lax.dot_general(query, ks[low:high, :], contract, preferred_element_type=jnp.float32)
+            own = jnp.where(causal, own, NEG)
+            top = jnp.max(own, axis=1, keepdims=True)
+            if number:
+                past = lax.dot_general(
+                    query, ks[0:low, :], contract, preferred_element_type=jnp.float32
+                )
+                top = jnp.maximum(top, jnp.max(past, axis=1, keepdims=True))
+            own = jnp.exp2((own - top) * EXP_SCALE)
+            total = jnp.sum(own, axis=1, keepdims=True)
+            result = jnp.dot(
+                own.astype(jnp.bfloat16), vs[low:high, :], preferred_element_type=jnp.float32
+            )
+            if number:
+                past = jnp.exp2((past - top) * EXP_SCALE)
+                total = total + jnp.sum(past, axis=1, keepdims=True)
+                result = result + jnp.dot(
+                    past.astype(jnp.bfloat16), vs[0:low, :], preferred_element_type=jnp.float32
+                )
+            ob[low:high, :] = (result / total).astype(jnp.bfloat16)
+            give(2 * number + 1, True)
+            give(2 * number, True)
+
+    @pl.loop(0, HEADS_HERE)
+    def _(step):
+        scatter(step, False)
+
+    @pl.when(active)
+    def _():
+        for block in range(N_CTX):
+            give(block, False)
+
+    pltpu.make_async_copy(out_ref, out_ref, out_recv).wait()
+
+
+def attend(queries, keys, values):
+    rows, width = queries.shape
+    length = rows * N_CTX
+    return pl.pallas_call(
+        attention_kernel,
+        out_shape=jax.ShapeDtypeStruct((rows, width), jnp.bfloat16),
+        in_specs=[pl.BlockSpec(memory_space=pl.ANY)] * 3,
+        out_specs=pl.BlockSpec(memory_space=pltpu.VMEM),
+        scratch_shapes=[
+            pltpu.VMEM((length, HD), jnp.bfloat16),
+            pltpu.VMEM((length, HD), jnp.bfloat16),
+            pltpu.VMEM((length, HD), jnp.bfloat16),
+            pltpu.VMEM((length, HD), jnp.bfloat16),
+            pltpu.SemaphoreType.DMA((3,)),
+            pltpu.SemaphoreType.DMA((HEADS_HERE, 3)),
+            pltpu.SemaphoreType.DMA((N_CTX,)),
+            pltpu.SemaphoreType.DMA,
+        ],
+        compiler_params=pltpu.CompilerParams(
+            collective_id=0, has_side_effects=True, vmem_limit_bytes=48 * 1024 * 1024
+        ),
+        cost_estimate=pl.CostEstimate(
+            flops=2 * length * length * HD, bytes_accessed=10**6, transcendentals=length * length // 2
+        ),
+    )(queries, keys, values)
 
 
 def activate(rows_in, gate_mat, up_mat, gate_scale, up_scale):
@@ -37,41 +209,10 @@
     scale_out,
 ):
     tok_rows = queries.shape[0]
-    quarter = queries.shape[1]
-    heads_here = quarter // HD
     n_dp = lax.axis_size("dp")
     n_tensor = lax.axis_size("tensor")
-    inv_root = 1.0 / math.sqrt(HD)
-    query_heads = queries.reshape(tok_rows, heads_here, HD)
-    query_pos = lax.axis_index("context") * tok_rows + jnp.arange(tok_rows, dtype=jnp.int32)
-    running_max = jnp.full((heads_here, tok_rows), NEG, jnp.float32)
-    key_shard = lax.all_gather(keys, "context", axis=0, tiled=True)
-    value_shard = lax.all_gather(values, "context", axis=0, tiled=True)
-    length = key_shard.shape[0]
-    key_heads = key_shard.reshape(length, heads_here, HD)
-    value_heads = value_shard.reshape(length, heads_here, HD)
-    scores = (
-        jnp.einsum("qhd,khd->hqk", query_heads, key_heads, preferred_element_type=jnp.float32)
-        * inv_root
-    )
-    key_pos = jnp.arange(length, dtype=jnp.int32)
-    allowed = (query_pos[:, None] >= key_pos[None, :])[None]
-    new_max = jnp.maximum(running_max, jnp.max(jnp.where(allowed, scores, NEG), axis=2))
-    weights = jnp.where(allowed, jnp.exp(scores - new_max[:, :, None]), 0.0)
-    new_sum = jnp.sum(weights, axis=2)
-    contrib = jnp.einsum(
-        "hqk,khd->hqd",
-        weights.astype(jnp.bfloat16),
-        value_heads,
-        preferred_element_type=jnp.float32,
-    )
-    attended = (
-        (contrib / new_sum[:, :, None])
-        .transpose(1, 0, 2)
-        .reshape(tok_rows, quarter)
-        .astype(jnp.bfloat16)
-    )
-    hidden_state = residual.astype(jnp.float32) + lax.optimization_barrier(attended).astype(
+    attended = attend(queries, keys, values)
+    hidden_state = residual.astype(jnp.float32) + attended.astype(
         jnp.float32
     )
     square_total = lax.psum(jnp.sum(hidden_state * hidden_state, axis=1), "tensor")

time: 641 us -> 498 us (0.78)
  waiting for transfers between devices: 333 us -> 176 us
  Pallas kernels: 0 us -> 44 us
  matrix products: 47.5 us -> 34.6 us
  local copies, waits for them, and re-layouts: 69.1 us -> 56.2 us
    all_gather x2 -> x0, waiting for transfers between devices: 160 us -> none  [the longest x1 93.4 us: local(): key_shard = lax.all_gather(keys, 'context', axis=0, tiled=True)]
    pallas_call x0 -> x1, Pallas kernels: none -> 44 us  [attend(): pl.pallas_call(attention_kernel, out_shape=jax.ShapeDtypeStruct((rows, wi...]
    dot_general x2 -> x0, matrix products: 12.8 us -> none  [the longest x1 8.13 us: local(): jnp.einsum('hqk,khd->hqd', weights.astype(jnp.bfloat16), value_heads, pre...]
    all_gather x1 -> x0, local copies, waits for them, and re-layouts: 6.68 us -> none  [local(): value_shard = lax.all_gather(values, 'context', axis=0, tiled=True)]
    unnamed x29 -> x35, local copies, waits for them, and re-layouts: 40.2 us -> 35.9 us
    unnamed x7 -> x5, waiting for transfers between devices: 36.2 us -> 35.4 us
  transfers between devices with their start and end apart: 7 -> 5, of which waited for: 7 -> 5; matrix products, arithmetic and copies ran while one was open for 5% -> 5% of each run, Pallas kernels for 0% -> 0%
where the time goes in v1:
time: 498 us; the launch traced here: 496 us
  waiting for transfers between devices  176 us (35%)
  blocking collectives  152 us (31%)
  local copies, waits for them, and re-layouts  56.2 us (11%)
  Pallas kernels  44 us (9%)
  matrix products  34.6 us (7%)
  between operations  13.9 us (3%)
  other arithmetic  12.8 us (3%)
  starting transfers between devices  6.69 us (1%)
    unnamed x1, blocking collectives  123 us
    all_gather x1, waiting for transfers between devices, local(): lax.all_gather(expert_rows, 'context', axis=0, tiled=True)  121 us
    pallas_call x1, Pallas kernels, attend(): pl.pallas_call(attention_kernel, out_shape=jax.ShapeDtypeStruct((rows, wi...  44 us
    unnamed x35, local copies, waits for them, and re-layouts  35.9 us
    unnamed x5, waiting for transfers between devices  35.4 us
    all_to_all x1, blocking collectives, local(): lax.all_to_all(outgoing, 'dp', split_axis=0, concat_axis=0, tiled=True)  18.6 us
    dot_general x1, matrix products, local(): jnp.dot(activated, w_down[0], preferred_element_type=jnp.float32)  16.8 us
    all_gather x1, waiting for transfers between devices, local(): widened = lax.all_gather(normed, 'tensor', axis=1, tiled=True)  11.8 us
  transfers between devices with their start and end apart: 5, of which 5 were waited for; matrix products, arithmetic and copies ran while one was open for 5% of the time, Pallas kernels for 0%

profile of v1, /device:TPU:8, one launch (start us, length us, event | category | flops | bytes accessed | tf_op | source)
XLA Modules:
  0.0 496.3 jit_solution(17782532116289654206)
XLA Ops:
  9.6 44.0 %shard_map.118 = bf16[128,1152]{1,0:T(8,128)(2,1)S(1)} custom-call(bf16[128,1152]{1,0:T(8,128)(2,1)S(1)} %copy-done.2, bf16[128,1152]{1,0:T(8,128)(2,1)S(1)} %copy-done.3, bf16[128,1152]{1,0:T(8,128)(2,1)S(1)} %copy-done.4), custom_call_target="tpu_custom_call" | custom-call | flops 1073741824 | bytes 1000000 | tf_op jit(solution)/shard_map/pallas_call | solution.py:167
  54.5 11.1 %psum.7 = f32[128]{0:T(128)} all-reduce(f32[128]{0:T(128)S(1)} %multiply_reduce_fusion), channel_id=1, replica_groups=mesh['dp'=4,'context'=16,'tensor'=4] {'tensor'}, use_global_device_ids=true, to_apply=%region_4.5 | all-reduce | flops 128 | bytes 1024 | tf_op jit(solution)/shard_map/psum | solution.py:218
  83.4 11.8 %all-gather.4.cloned.1.call-done = bf16[128,4608]{1,0:T(8,128)(2,1)} async-done(((bf16[128,1152]{1,0:T(8,128)(2,1)}), bf16[128,4608]{1,0:T(8,128)(2,1)}) %all-gather.4.cloned.1.call-update) | async-done | bytes 1179664 | tf_op jit(solution)/shard_map/all_gather | solution.py:240
  95.2 2.4 convolution_convert_fusion.2
  97.7 2.2 all_to_all.16
  99.9 18.6 %all_to_all.24 = bf16[4,17,4608]{2,1,0:T(8,128)(2,1)} all-to-all(bf16[4,17,4608]{2,1,0:T(8,128)(2,1)} %all_to_all.16), channel_id=1, replica_groups=mesh['dp'=4,'context'=16,'tensor'=4] {'dp'}, dimensions={0} | all-to-all | bytes 1253376 | tf_op jit(solution)/shard_map/all_to_all | solution.py:245
  118.5 2.2 reshape.70
  120.8 121.5 %all-gather.6.cloned.1.call-done = bf16[16,68,4608]{2,1,0:T(8,128)(2,1)} async-done(((bf16[1,68,4608]{2,1,0:T(8,128)(2,1)}), bf16[16,68,4608]{2,1,0:T(8,128)(2,1)}) %all-gather.6.cloned.1.call-update) | async-done | bytes 10027024 | tf_op jit(solution)/shard_map/all_gather | solution.py:247
  242.3 10.7 %reshape.71 = bf16[1088,4608]{1,0:T(8,128)(2,1)} reshape(bf16[16,68,4608]{2,1,0:T(8,128)(2,1)} %all-gather.6.cloned.1.call-done) | data formatting | bytes 20054016
  253.0 9.9 %fusion.6 = f32[1088,384]{1,0:T(8,128)} fusion(bf16[1088,4608]{1,0:T(8,128)(2,1)} %reshape.71, bf16[1,4608,384]{2,1,0:T(8,128)(2,1)} %param.19, f32[384]{0:T(512)S(1)} %get-tuple-element.6), kind=kOutput, calls=%fused_computation.8 | convolution fusion | flops 3850788864 | bytes 15238656 | tf_op jit(solution)/shard_map/dot_general | solution.py:192
  262.9 16.8 %convolution_convert_fusion = bf16[1088,4608]{1,0:T(8,128)(2,1)} fusion(bf16[1,384,4608]{2,1,0:T(8,128)(2,1)S(1)} %copy-done, bf16[1088,4608]{1,0:T(8,128)(2,1)} %reshape.71, bf16[1,4608,384]{2,1,0:T(8,128)(2,1)} %param.20, f32[1088,384]{1,0:T(8,128)} %fusion.6, f32[384]{0:T(512)S(1)} %get-tuple-element.5), kind=kOutput, calls=%fused_computation | convolution fusion | flops 7708680192 | bytes 28804608 | tf_op jit(solution)/shard_map/dot_general | solution.py:254
  279.7 122.8 %fusion = bf16[72,4608]{1,0:T(8,128)(2,1)} fusion(bf16[1088,4608]{1,0:T(8,128)(2,1)} %convolution_convert_fusion), kind=kCustom, calls=%all-reduce-scatter | all-reduce-scatter fusion | flops 5308417 | bytes 10691584
  402.4 2.0 slice.17
  404.5 2.4 collective-permute-start
  409.6 13.1 %collective-permute-done = bf16[60,4608]{1,0:T(8,128)(2,1)} collective-permute-done((bf16[60,4608]{1,0:T(8,128)(2,1)}, bf16[60,4608]{1,0:T(8,128)(2,1)}, u32[]{:S(2)}, u32[]{:S(2)}) %collective-permute-start) | collective-permute-done | bytes 552992
  422.7 10.2 %concatenate = bf16[132,4608]{1,0:T(8,128)(2,1)} concatenate(bf16[60,4608]{1,0:T(8,128)(2,1)} %collective-permute-done, bf16[72,4608]{1,0:T(8,128)(2,1)} %fusion), dimensions={0} | concatenate | bytes 2433024
  432.8 2.2 multiply_convert_fusion
  435.0 2.2 all_to_all.19
  437.3 4.2 all-to-all-start.1
  448.9 6.8 %all-to-all-done.1 = bf16[4,17,4608]{2,1,0:T(8,128)(2,1)} async-done(((bf16[4,17,4608]{2,1,0:T(8,128)(2,1)}), bf16[4,17,4608]{2,1,0:T(8,128)(2,1)}, u32[]{:S(2)}, u32[]{:S(2)}) %all-to-all-start.1) | async-done | bytes 626720 | tf_op jit(solution)/shard_map/all_to_all | solution.py:260
  455.8 2.2 all_to_all.21
  458.0 3.2 convolution_convert_fusion.1
  461.2 2.4 copy.21
  463.6 22.3 %reduce-scatter.6.cloned.1.call-done = bf16[1152,128]{1,0:T(8,128)(2,1)} async-done(((bf16[4608,128]{1,0:T(8,128)(2,1)}), bf16[1152,128]{1,0:T(8,128)(2,1)}) %reduce-scatter.6.cloned.1.call-update) | async-done | bytes 294928
  (60 shorter events, 35.0 us)
Async XLA Ops:
  6.5 256.4 %copy-start = (bf16[1,384,4608]{2,1,0:T(8,128)(2,1)S(1)}, bf16[1,384,4608]{2,1,0:T(8,128)(2,1)}, u32[]{:S(2)}) copy-start(bf16[1,384,4608]{2,1,0:T(8,128)(2,1)} %param.21) | copy-start | bytes 10616836
  6.5 88.7 %all-gather.4.cloned.1.call-start = ((), (), s32[]{:S(2)}) async-start(), calls=%async_computation.3 | async-start | bytes 1474560 | tf_op jit(solution)/shard_map/all_gather | solution.py:240
  6.5 1.1 copy-start.2
  7.7 1.0 copy-start.3
  8.7 1.0 copy-start.4
  9.6 44.7 %copy-start.5 = (bf16[128,1152]{1,0:T(8,128)(2,1)S(1)}, bf16[128,1152]{1,0:T(8,128)(2,1)}, u32[]{:S(2)}) copy-start(bf16[128,1152]{1,0:T(8,128)(2,1)} %param.15) | copy-start | bytes 884740
  9.6 56.7 %copy-start.6 = (f32[1152]{0:T(1024)S(1)}, f32[1152]{0:T(1024)}, u32[]{:S(2)}) copy-start(f32[1152]{0:T(1024)} %param.16) | copy-start | bytes 13828
  9.6 58.6 %copy-start.8 = (s32[128,2]{0,1:T(2,128)S(1)}, s32[128,2]{0,1:T(2,128)}, u32[]{:S(2)}) copy-start(s32[128,2]{0,1:T(2,128)} %param.17) | copy-start | bytes 3076
  53.6 0.7 copy-start.1
  68.2 174.1 %all-gather.6.cloned.1.call-start = ((), (), s32[]{:S(2)}) async-start(), calls=%async_computation.4 | async-start | bytes 11280384 | tf_op jit(solution)/shard_map/all_gather | solution.py:247
  77.6 0.6 copy-start.10
  99.9 20.9 %copy-start.7 = (f32[1,2,384]{2,1,0:T(2,128)S(1)}, f32[1,2,384]{2,1,0:T(2,128)}, u32[]{:S(2)}) copy-start(f32[1,2,384]{2,1,0:T(2,128)} %param.22) | copy-start | bytes 9220
  279.7 128.6 %copy-start.12 = (u32[256]{0:T(256)S(1)}, u32[256]{0:T(256)}, u32[]{:S(2)}) copy-start(u32[256]{0:T(256)} %constant.54) | copy-start | bytes 3076
  404.5 18.2 %collective-permute-start = (bf16[60,4608]{1,0:T(8,128)(2,1)}, bf16[60,4608]{1,0:T(8,128)(2,1)}, u32[]{:S(2)}, u32[]{:S(2)}) collective-permute-start(bf16[60,4608]{1,0:T(8,128)(2,1)} %slice.17), channel_id=1, source_target_pairs={{0,4},{4,8},{8,12},{12,16},{16,20},{20,24},{24,28},{28,32},{32,36}... | collective-permute-start | bytes 1658888
  432.8 8.7 %copy-start.9 = (f32[128,2]{0,1:T(2,128)S(1)}, f32[128,2]{0,1:T(2,128)}, u32[]{:S(2)}) copy-start(f32[128,2]{0,1:T(2,128)} %param.18) | copy-start | bytes 3076
  432.8 10.4 %copy-start.11 = (s32[256]{0:T(256)S(1)}, s32[256]{0:T(256)}, u32[]{:S(2)}) copy-start(s32[256]{0:T(256)} %copy-done.10) | copy-start | bytes 3076
  437.3 18.5 %all-to-all-start.1 = ((bf16[4,17,4608]{2,1,0:T(8,128)(2,1)}), bf16[4,17,4608]{2,1,0:T(8,128)(2,1)}, u32[]{:S(2)}, u32[]{:S(2)}) async-start(bf16[4,17,4608]{2,1,0:T(8,128)(2,1)} %all_to_all.19), calls=%async_computation.1 | async-start | bytes 1769472 | tf_op jit(solution)/shard_map/all_to_all | solution.py:260
  441.5 44.5 %reduce-scatter.6.cloned.1.call-start = ((), (), s32[]{:S(2)}) async-start(), calls=%async_computation.5 | async-start | bytes 1474560
Sparse Core Ops, SparseCore 0:
  68.3 26.8 all-gather.3
  120.9 121.3 all-gather.5
  463.8 22.1 reduce-scatter.5

commit v2 on v1

--- a/solution.py
+++ b/solution.py
@@ -10,14 +10,8 @@
 D = 4608
 HD = 128
 EXPERTS = 16
-TOP = 2
-CAP = 17
-
-
 EPS = 1e-06
 NEG = -1e30
-
-
 N_CTX = 16
 HEADS_HERE = 9
 MESH = pl.DeviceIdType.MESH
@@ -29,10 +23,28 @@
 
 
 def attention_kernel(
-    q_ref, k_ref, v_ref, out_ref, qs, ks, vs, ob, recv_sem, send_sem, out_send, out_recv
+    q_ref,
+    k_ref,
+    v_ref,
+    gate_ref,
+    out_ref,
+    gate_out,
+    qs,
+    ks,
+    vs,
+    ob,
+    recv_sem,
+    send_sem,
+    out_send,
+    out_recv,
+    gate_send,
+    gate_recv,
 ):
     ctx = lax.axis_index("context")
-    core = lax.rem(lax.axis_index("dp"), 2)
+    dp = lax.axis_index("dp")
+    core = lax.rem(dp, 2)
+    swapping = core != lax.div(ctx, N_CTX // 2)
+    diagonal = {"dp": dp + 1 - 2 * core, "context": lax.rem(ctx + N_CTX // 2, N_CTX)}
     rows = q_ref.shape[0]
 
     barrier = pltpu.get_barrier_semaphore()
@@ -43,7 +55,16 @@
             barrier, inc=1, device_id={"context": lax.rem(ctx + step, N_CTX)}, device_id_type=MESH
         )
 
-    pl.semaphore_wait(barrier, N_CTX - 1)
+    pl.semaphore_signal(barrier, inc=1, device_id=diagonal, device_id_type=MESH)
+    pl.semaphore_wait(barrier, N_CTX)
+    swap = pltpu.make_async_remote_copy(
+        src_ref=gate_ref,
+        dst_ref=gate_out,
+        send_sem=gate_send,
+        recv_sem=gate_recv,
+        device_id=diagonal,
+        device_id_type=MESH,
+    )
 
     my_rows = pl.ds(pl.multiple_of(ctx * rows, rows), rows)
     sources = (k_ref, q_ref, v_ref)
@@ -81,6 +102,10 @@
     @pl.loop(0, HEADS_HERE)
     def _(step):
         scatter(step, True)
+
+    @pl.when(swapping)
+    def _():
+        swap.start()
 
     base = lax.rem(ctx + 8 * core, N_CTX)
     my_head = lax.div(base * HEADS_HERE + N_CTX - 1, N_CTX)
@@ -160,15 +185,22 @@
 
     pltpu.make_async_copy(out_ref, out_ref, out_recv).wait()
 
-
-def attend(queries, keys, values):
+    @pl.when(swapping)
+    def _():
+        swap.wait()
+
+
+def attend(queries, keys, values, w_gate):
     rows, width = queries.shape
     length = rows * N_CTX
     return pl.pallas_call(
         attention_kernel,
-        out_shape=jax.ShapeDtypeStruct((rows, width), jnp.bfloat16),
-        in_specs=[pl.BlockSpec(memory_space=pl.ANY)] * 3,
-        out_specs=pl.BlockSpec(memory_space=pltpu.VMEM),
+        out_shape=(
+            jax.ShapeDtypeStruct((rows, width), jnp.bfloat16),
+            jax.ShapeDtypeStruct(w_gate.shape, jnp.bfloat16),
+        ),
+        in_specs=[pl.BlockSpec(memory_space=pl.ANY)] * 4,
+        out_specs=(pl.BlockSpec(memory_space=pltpu.VMEM), pl.BlockSpec(memory_space=pl.ANY)),
         scratch_shapes=[
             pltpu.VMEM((length, HD), jnp.bfloat16),
             pltpu.VMEM((length, HD), jnp.bfloat16),
@@ -178,6 +210,8 @@
             pltpu.SemaphoreType.DMA((HEADS_HERE, 3)),
             pltpu.SemaphoreType.DMA((N_CTX,)),
             pltpu.SemaphoreType.DMA,
+            pltpu.SemaphoreType.DMA,
+            pltpu.SemaphoreType.DMA,
         ],
         compiler_params=pltpu.CompilerParams(
             collective_id=0, has_side_effects=True, vmem_limit_bytes=48 * 1024 * 1024
@@ -185,13 +219,625 @@
         cost_estimate=pl.CostEstimate(
             flops=2 * length * length * HD, bytes_accessed=10**6, transcendentals=length * length // 2
         ),
-    )(queries, keys, values)
-
-
-def activate(rows_in, gate_mat, up_mat, gate_scale, up_scale):
-    gate_val = jnp.dot(rows_in, gate_mat, preferred_element_type=jnp.float32) * gate_scale
-    up_val = jnp.dot(rows_in, up_mat, preferred_element_type=jnp.float32) * up_scale
-    return (jax.nn.silu(gate_val) * up_val).astype(jnp.bfloat16)
+    )(queries, keys, values, w_gate)
+
+
+MAIN = 16
+TILE_ROWS = 16
+SLOT = 64
+OVER = 256
+GROUP = 16
+N_Z = 8
+OWN, SIB_OWN = 0, 1
+
+
+def major(k):
+    return 14 if k == 4 else 4 * k - 2
+
+
+def minor(k):
+    return 4 * k - 1
+
+
+def twin(slot):
+    return slot + 1 if slot in (0, 14) else slot + 2
+
+
+CARRIED = [OWN] + [s for k in (1, 2, 3) for s in (major(k), minor(k))] + [major(4)]
+STEPS = [(0, 2), (2, 4), (6, 4), (10, 4), (14, 2)]
+
+
+def arrived(ref, sem):
+    pltpu.make_async_copy(ref, ref, sem).wait()
+
+
+def one_hot(hit):
+    return jnp.where(hit, 1.0, 0.0).astype(jnp.bfloat16)
+
+
+def exact_dot(left, right):
+    return jnp.dot(left, right, preferred_element_type=jnp.float32)
+
+
+def iotas(rows, columns):
+    return (
+        lax.broadcasted_iota(jnp.int32, (rows, columns), 0),
+        lax.broadcasted_iota(jnp.int32, (rows, columns), 1),
+    )
+
+
+def expert_kernel(
+    residual_ref,
+    attended_ref,
+    gain_ref,
+    routes_ref,
+    routes_t_ref,
+    weight_ref,
+    gate_own,
+    gate_swapped,
+    up_own,
+    down_own,
+    wide_own,
+    tall_own,
+    out_ref,
+    xm,
+    xo,
+    ym,
+    yo,
+    sib_m,
+    sib_o,
+    rxa_m,
+    rxa_o,
+    rxb_m,
+    rxb_o,
+    w1,
+    wd,
+    wide,
+    tall,
+    act,
+    hid,
+    hidden,
+    disp_m,
+    disp_o,
+    eo_m,
+    eo_o,
+    ret_m,
+    ret_o,
+    over_x,
+    over_y,
+    spread,
+    gather,
+    squares,
+    w_recv,
+    w_send,
+    sq_recv,
+    sq_send,
+    disp_recv,
+    disp_send,
+    aga_recv,
+    aga_send,
+    agb_recv,
+    agb_send,
+    sibx_recv,
+    sibx_send,
+    siby_recv,
+    siby_send,
+    rsa_recv,
+    rsa_send,
+    rsb_recv,
+    rsb_send,
+    ret_recv,
+    ret_send,
+):
+    dp, ctx, tensor = lax.axis_index("dp"), lax.axis_index("context"), lax.axis_index("tensor")
+    core, y_hi = lax.rem(dp, 2), lax.div(dp, 2)
+    z, y_lo = lax.rem(ctx, N_Z), lax.div(ctx, N_Z)
+    sign = 1 - 2 * core
+    place = y_hi * 2 + y_lo
+    rank = place * 4 + tensor
+    rows, quarter = residual_ref.shape
+    width = xm.shape[1]
+    hid_dev = wd.shape[0]
+
+    def member(number):
+        other = lax.div(number, 4)
+        return {
+            "dp": lax.div(other, 2) * 2 + core,
+            "context": lax.rem(other, 2) * N_Z + z,
+            "tensor": lax.rem(number, 4),
+        }
+
+    ahead = {"context": y_lo * N_Z + lax.rem(z + sign + N_Z, N_Z)}
+    behind = {"context": y_lo * N_Z + lax.rem(z - sign + N_Z, N_Z)}
+    sibling = {"dp": y_hi * 2 + 1 - core}
+    diagonal = {"dp": y_hi * 2 + 1 - core, "context": (1 - y_lo) * N_Z + z}
+
+    barrier = pltpu.get_barrier_semaphore()
+    for other in (ahead, behind, sibling, diagonal):
+        pl.semaphore_signal(barrier, inc=1, device_id=other, device_id_type=MESH)
+
+    @pl.loop(1, GROUP)
+    def _(step):
+        pl.semaphore_signal(
+            barrier, inc=1, device_id=member(lax.rem(rank + step, GROUP)), device_id_type=MESH
+        )
+
+    pl.semaphore_wait(barrier, GROUP + 3)
+
+    pending = []
+
+    def send(src, dst, send_sem, recv_sem, device):
+        copy = pltpu.make_async_remote_copy(
+            src_ref=src,
+            dst_ref=dst,
+            send_sem=send_sem,
+            recv_sem=recv_sem,
+            device_id=device,
+            device_id_type=MESH,
+        )
+        copy.start()
+        pending.append(copy)
+
+    swapping = core != y_lo
+    up_part = w1.at[:, pl.ds(hid_dev, hid_dev)]
+    gate_part = w1.at[:, pl.ds(0, hid_dev)]
+    moved = ((up_own, up_part), (down_own, wd), (wide_own, wide), (tall_own, tall))
+
+    def swap(index):
+        return pltpu.make_async_remote_copy(
+            src_ref=moved[index][0],
+            dst_ref=moved[index][1],
+            send_sem=w_send.at[index],
+            recv_sem=w_recv.at[index],
+            device_id=diagonal,
+            device_id_type=MESH,
+        )
+
+    @pl.when(swapping)
+    def _():
+        for index in (2, 3, 0, 1):
+            swap(index).start()
+        pltpu.make_async_copy(gate_swapped, gate_part, w_recv.at[4]).start()
+
+    @pl.when(jnp.logical_not(swapping))
+    def _():
+        for index in (2, 3, 0, 1):
+            pltpu.make_async_copy(moved[index][0], moved[index][1], w_recv.at[index]).start()
+        pltpu.make_async_copy(gate_own, gate_part, w_recv.at[4]).start()
+
+    state = residual_ref[...].astype(jnp.float32) + attended_ref[...].astype(jnp.float32)
+    hidden[...] = state
+    own_squares = jnp.sum(state * state, axis=1, keepdims=True)
+    squares[tensor] = jnp.broadcast_to(own_squares, (rows, rows)).T[0:8, :]
+
+    def tell(step):
+        peer = lax.rem(tensor + step, 4)
+        return pltpu.make_async_remote_copy(
+            src_ref=squares.at[tensor],
+            dst_ref=squares.at[tensor],
+            send_sem=sq_send.at[peer],
+            recv_sem=sq_recv.at[tensor],
+            device_id={"tensor": peer},
+            device_id_type=MESH,
+        )
+
+    for step in (1, 2, 3):
+        tell(step).start()
+
+    row, col = iotas(EXPERTS, rows)
+    named = jnp.logical_or(row == routes_t_ref[0:1, :], row == routes_t_ref[1:2, :])
+    first, second = iotas(rows, rows)
+    ranks = exact_dot(one_hot(named), one_hot(first < second))
+    ranks = jnp.where(named, ranks, -1.0)
+    row, col = iotas(EXPERTS * MAIN, EXPERTS)
+    widened = exact_dot(one_hot((row >> 4) == col), ranks.astype(jnp.bfloat16))
+    row, col = iotas(EXPERTS * MAIN, rows)
+    pick_main = one_hot(widened == (row & 15).astype(jnp.float32))
+    pick_over = one_hot(ranks == float(MAIN))
+
+    for step in (1, 2, 3):
+        peer = lax.rem(tensor + step, 4)
+        arrived(squares.at[peer], sq_recv.at[peer])
+    total = squares[0] + squares[1] + squares[2] + squares[3]
+    inverse = lax.rsqrt(total / D + EPS)
+    inverse = jnp.broadcast_to(inverse[0:1, :], (rows, rows)).T[:, 0:1]
+    normed = (hidden[...] * inverse * gain_ref[...]).astype(jnp.bfloat16)
+    disp_m[...] = exact_dot(pick_main, normed).astype(jnp.bfloat16)
+    overflow = exact_dot(pick_over, normed).astype(jnp.bfloat16)
+    pieces = quarter // HD
+    stacked = jnp.concatenate(
+        [overflow[:, n * HD : (n + 1) * HD] for n in range(pieces)], axis=0
+    )
+    row, col = iotas(EXPERTS * TILE_ROWS, EXPERTS * pieces)
+    shuffle = one_hot((((col & 15) << 4) | (col >> 4)) == row)
+    disp_o[...] = exact_dot(shuffle, stacked).astype(jnp.bfloat16)
+
+    def rows_of(number):
+        return pl.ds(pl.multiple_of(number * TILE_ROWS, TILE_ROWS), TILE_ROWS)
+
+    def columns_of(number):
+        return pl.ds(pl.multiple_of(number * quarter, quarter), quarter)
+
+    def dispatch(step):
+        other = lax.rem(rank + step, GROUP)
+        pairs = (
+            (disp_m.at[rows_of(other), :], xm.at[rows_of(place), columns_of(tensor)]),
+            (disp_o.at[rows_of(other), :], xo.at[rows_of(rank), :]),
+        )
+        return [
+            pltpu.make_async_remote_copy(
+                src_ref=src,
+                dst_ref=dst,
+                send_sem=disp_send.at[step, index],
+                recv_sem=disp_recv.at[index],
+                device_id=member(other),
+                device_id_type=MESH,
+            )
+            for index, (src, dst) in enumerate(pairs)
+        ]
+
+    pltpu.make_async_copy(
+        disp_m.at[rows_of(rank), :], xm.at[rows_of(place), columns_of(tensor)], disp_recv.at[0]
+    ).start()
+    pltpu.make_async_copy(
+        disp_o.at[rows_of(rank), :], xo.at[rows_of(rank), :], disp_recv.at[1]
+    ).start()
+
+    @pl.loop(1, GROUP)
+    def _(step):
+        for copy in dispatch(step):
+            copy.start()
+
+    row, col = iotas(36 * 16, 4 * OVER)
+    chunk, inside = col >> 8, col & 255
+    source, part, piece = inside >> 6, (inside >> 4) & 3, inside & 15
+    goal = (part * pieces + piece) * 16 + chunk * 4 + source
+    spread[...] = one_hot(jnp.logical_and(piece < pieces, goal == row))
+    row, col = iotas(4 * OVER, 36 * 16)
+    chunk, inside = row >> 8, row & 255
+    source, part, piece = inside >> 6, (inside >> 4) & 3, inside & 15
+    goal = (part * pieces + piece) * 16 + chunk * 4 + source
+    gather[...] = one_hot(jnp.logical_and(piece < pieces, goal == col))
+
+    def main(slot):
+        return pl.ds(slot * SLOT, SLOT)
+
+    def over(slot):
+        return pl.ds(slot * OVER, OVER)
+
+    def pass_on(slot, goal, send_sem, recv_sem, number, device):
+        send(xm.at[main(slot), :], xm.at[main(goal), :], send_sem.at[number, 0], recv_sem.at[number, 0], device)
+        send(xo.at[over(slot), :], xo.at[over(goal), :], send_sem.at[number, 1], recv_sem.at[number, 1], device)
+
+    def landed(slot, recv_sem, number):
+        arrived(xm.at[main(slot), :], recv_sem.at[number, 0])
+        arrived(xo.at[over(slot), :], recv_sem.at[number, 1])
+
+    def share(slot):
+        pass_on(slot, twin(slot), sibx_send, sibx_recv, CARRIED.index(slot), sibling)
+
+    arrived(xm.at[main(OWN), :], disp_recv.at[0])
+    arrived(xo.at[over(OWN), :], disp_recv.at[1])
+    pass_on(OWN, major(1), aga_send, aga_recv, 0, ahead)
+    pass_on(OWN, minor(1), agb_send, agb_recv, 0, behind)
+    share(OWN)
+    for k in (1, 2, 3):
+        landed(major(k), aga_recv, k - 1)
+        pass_on(major(k), major(k + 1), aga_send, aga_recv, k, ahead)
+        share(major(k))
+        landed(minor(k), agb_recv, k - 1)
+        if k < 3:
+            pass_on(minor(k), minor(k + 1), agb_send, agb_recv, k, behind)
+        share(minor(k))
+
+    def fetch_shared(step):
+        low, count = STEPS[step]
+        for slot in CARRIED:
+            if low <= slot < low + count:
+                landed(twin(slot), sibx_recv, CARRIED.index(slot))
+
+    def step_rows(step):
+        return STEPS[step][1] * SLOT
+
+    def hidden_part(step):
+        low, count = STEPS[step]
+        size = step_rows(step)
+        tiles = xo[low * OVER : (low + count) * OVER, :]
+        stack = exact_dot(spread[:, 0 : count * OVER], tiles).astype(jnp.bfloat16)
+        for n in range(36):
+            over_x[:, n * HD : (n + 1) * HD] = stack[n * 16 : (n + 1) * 16, :]
+
+        @pl.loop(0, 3)
+        def _(n):
+            lanes = pl.ds(pl.multiple_of(n * 256, 256), 256)
+            rows_in = jnp.concatenate([xm[low * SLOT : low * SLOT + size, :], over_x[...]], axis=0)
+            hid[0 : size + 16, lanes] = exact_dot(rows_in, w1[:, lanes])
+
+        for n in range(hid_dev // HD):
+            lanes = slice(n * HD, (n + 1) * HD)
+            gate = hid[0 : size + 16, lanes] * tall[n : n + 1, :]
+            up = hid[0 : size + 16, hid_dev + n * HD : hid_dev + (n + 1) * HD] * tall[n + 3 : n + 4, :]
+            act[step * 272 : step * 272 + size + 16, lanes] = (
+                gate / (1.0 + jnp.exp(-gate)) * up
+            ).astype(jnp.bfloat16)
+
+    def down_part(step):
+        low, count = STEPS[step]
+        size = step_rows(step)
+
+        @pl.loop(0, width // 512)
+        def _(n):
+            lanes = pl.ds(pl.multiple_of(n * 512, 512), 512)
+            result = exact_dot(act[step * 272 : step * 272 + size + 16, :], wd[:, lanes])
+            result = result.astype(jnp.bfloat16)
+            ym[low * SLOT : low * SLOT + size, lanes] = result[0:size, :]
+            over_y[:, lanes] = result[size:, :]
+
+        stack = jnp.concatenate([over_y[:, n * HD : (n + 1) * HD] for n in range(36)], axis=0)
+        yo[low * OVER : (low + count) * OVER, :] = exact_dot(
+            gather[0 : count * OVER, :], stack
+        ).astype(jnp.bfloat16)
+        for slot in CARRIED:
+            if low <= slot < low + count:
+                number = CARRIED.index(slot)
+                other = twin(slot)
+                send(ym.at[main(other), :], sib_m.at[number], siby_send.at[number, 0], siby_recv.at[number, 0], sibling)
+                send(yo.at[over(other), :], sib_o.at[number], siby_send.at[number, 1], siby_recv.at[number, 1], sibling)
+
+    arrived(gate_part, w_recv.at[4])
+    arrived(up_part, w_recv.at[0])
+    arrived(wide, w_recv.at[2])
+    arrived(tall, w_recv.at[3])
+    for step in (0, 1, 2, 3):
+        fetch_shared(step)
+        hidden_part(step)
+    landed(major(4), aga_recv, 3)
+    share(major(4))
+    fetch_shared(4)
+    hidden_part(4)
+    arrived(wd, w_recv.at[1])
+
+    def add_up(slot, extras):
+        number = CARRIED.index(slot)
+        arrived(sib_m.at[number], siby_recv.at[number, 0])
+        arrived(sib_o.at[number], siby_recv.at[number, 1])
+
+        def summed(own, others):
+            value = own.astype(jnp.float32)
+            for other in others:
+                value = value + other.astype(jnp.float32)
+            return value
+
+        def block(lanes):
+            return summed(
+                ym[main(slot), lanes],
+                [sib_m[number, :, lanes]] + [ref[place, :, lanes] for ref, _, place in extras],
+            )
+
+        tiles = summed(
+            yo[over(slot), :], [sib_o[number]] + [ref[place] for _, ref, place in extras]
+        )
+        return block, tiles
+
+    def hop(slot, extras, goal_m, goal_o, send_sem, recv_sem, number, device):
+        for ref_m, ref_o, place, sems in extras:
+            arrived(ref_m.at[place], sems.at[place, 0])
+            arrived(ref_o.at[place], sems.at[place, 1])
+        block, tiles = add_up(slot, [e[:3] for e in extras])
+
+        @pl.loop(0, width // 512)
+        def _(n):
+            lanes = pl.ds(pl.multiple_of(n * 512, 512), 512)
+            ym[main(slot), lanes] = block(lanes).astype(jnp.bfloat16)
+
+        send(ym.at[main(slot), :], goal_m.at[number], send_sem.at[number, 0], recv_sem.at[number, 0], device)
+        yo[over(slot), :] = tiles.astype(jnp.bfloat16)
+        send(yo.at[over(slot), :], goal_o.at[number], send_sem.at[number, 1], recv_sem.at[number, 1], device)
+
+    def hop_a(k):
+        extras = [(rxa_m, rxa_o, k, rsa_recv)] if k < 4 else []
+        hop(major(k), extras, rxa_m, rxa_o, rsa_send, rsa_recv, k - 1, behind)
+
+    def hop_b(k):
+        extras = [(rxb_m, rxb_o, k, rsb_recv)] if k < 3 else []
+        hop(minor(k), extras, rxb_m, rxb_o, rsb_send, rsb_recv, k - 1, ahead)
+
+    down_part(4)
+    hop_a(4)
+    down_part(3)
+    hop_b(3)
+    down_part(2)
+    down_part(1)
+    down_part(0)
+    hop_a(3)
+    hop_b(2)
+    hop_a(2)
+    hop_b(1)
+    hop_a(1)
+    last = [(rxb_m, rxb_o, 0, rsb_recv), (rxa_m, rxa_o, 0, rsa_recv)]
+    for ref_m, ref_o, spot, sems in last:
+        arrived(ref_m.at[spot], sems.at[spot, 0])
+        arrived(ref_o.at[spot], sems.at[spot, 1])
+    block, tiles = add_up(OWN, [e[:3] for e in last])
+
+    @pl.loop(0, width // 512)
+    def _(n):
+        lanes = pl.ds(pl.multiple_of(n * 512, 512), 512)
+        eo_m[:, lanes] = (block(lanes) * wide[0:1, lanes]).astype(jnp.bfloat16)
+
+    for n in range(4):
+        eo_o[n * 64 : (n + 1) * 64, :] = (tiles[n * 64 : (n + 1) * 64, :] * tall[8:72, :]).astype(
+            jnp.bfloat16
+        )
+
+    def give_back(step):
+        other = lax.rem(rank + step, GROUP)
+        to_place, to_part = lax.div(other, 4), lax.rem(other, 4)
+        pairs = (
+            (eo_m.at[rows_of(to_place), columns_of(to_part)], ret_m.at[rows_of(rank), :]),
+            (eo_o.at[rows_of(other), :], ret_o.at[rows_of(rank), :]),
+        )
+        return [
+            pltpu.make_async_remote_copy(
+                src_ref=src,
+                dst_ref=dst,
+                send_sem=ret_send.at[step, index],
+                recv_sem=ret_recv.at[index],
+                device_id=member(other),
+                device_id_type=MESH,
+            )
+            for index, (src, dst) in enumerate(pairs)
+        ]
+
+    pltpu.make_async_copy(
+        eo_m.at[rows_of(place), columns_of(tensor)], ret_m.at[rows_of(rank), :], ret_recv.at[0]
+    ).start()
+    pltpu.make_async_copy(
+        eo_o.at[rows_of(rank), :], ret_o.at[rows_of(rank), :], ret_recv.at[1]
+    ).start()
+
+    @pl.loop(1, GROUP)
+    def _(step):
+        for copy in give_back(step):
+            copy.start()
+
+    expert_id = iotas(rows, EXPERTS)[1]
+    hits = [expert_id == routes_ref[:, k : k + 1] for k in range(2)]
+    first, second = iotas(rows, rows)
+    both = one_hot(jnp.logical_or(hits[0], hits[1]))
+    token_ranks = exact_dot(one_hot(second < first), both)
+    row, col = iotas(EXPERTS, EXPERTS * MAIN)
+    expand = one_hot((col >> 4) == row)
+    slot_rank = (iotas(rows, EXPERTS * MAIN)[1] & 15).astype(jnp.float32)
+    selects = []
+    for k in range(2):
+        own_ranks = jnp.where(hits[k], token_ranks, -1.0)
+        wide_ranks = exact_dot(own_ranks.astype(jnp.bfloat16), expand)
+        selects.append((one_hot(wide_ranks == slot_rank), one_hot(own_ranks == float(MAIN))))
+    row, col = iotas(EXPERTS * pieces, EXPERTS * TILE_ROWS)
+    unshuffle = one_hot((((row & 15) << 4) | (row >> 4)) == col)
+
+    arrived(ret_m, ret_recv.at[0])
+    arrived(ret_o, ret_recv.at[1])
+    back = exact_dot(unshuffle, ret_o[...]).astype(jnp.bfloat16)
+    back = jnp.concatenate(
+        [back[n * EXPERTS : (n + 1) * EXPERTS, :] for n in range(pieces)], axis=1
+    )
+    routed = jnp.zeros((rows, quarter), jnp.float32)
+    for k in range(2):
+        picked = exact_dot(selects[k][0], ret_m[...]) + exact_dot(selects[k][1], back)
+        routed = routed + picked * weight_ref[:, k : k + 1]
+    out_ref[...] = (hidden[...] + routed).astype(jnp.bfloat16)
+
+    for copy in pending:
+        copy.wait_send()
+    for step in (1, 2, 3):
+        tell(step).wait_send()
+
+    @pl.loop(1, GROUP)
+    def _(step):
+        for copy in dispatch(step) + give_back(step):
+            copy.wait_send()
+
+    @pl.when(swapping)
+    def _():
+        for index in range(4):
+            swap(index).wait_send()
+
+
+def experts(
+    residual, attended, norm_gain, routes, route_weight, gate_swapped, w_gate, w_up, w_down, scale_hidden, scale_out
+):
+    rows, quarter = residual.shape
+    width, hid_dev = w_gate.shape
+    wide = jnp.broadcast_to(scale_out, (8, width))
+    pieces = quarter // HD
+    tall = jnp.concatenate(
+        [
+            jnp.pad(scale_hidden.reshape(2 * hid_dev // HD, HD), ((0, 2), (0, 0))),
+            jnp.pad(scale_out.reshape(4, pieces, HD), ((0, 0), (0, 16 - pieces), (0, 0))).reshape(64, HD),
+        ],
+        axis=0,
+    )
+    vmem = pl.BlockSpec(memory_space=pltpu.VMEM)
+    hbm = pl.BlockSpec(memory_space=pl.ANY)
+    half = jnp.bfloat16
+    dma = pltpu.SemaphoreType.DMA
+    return pl.pallas_call(
+        expert_kernel,
+        out_shape=jax.ShapeDtypeStruct((rows, quarter), half),
+        in_specs=[vmem] * 6 + [hbm] * 6,
+        out_specs=vmem,
+        scratch_shapes=[
+            pltpu.VMEM((16 * SLOT, width), half),
+            pltpu.VMEM((16 * OVER, HD), half),
+            pltpu.VMEM((16 * SLOT, width), half),
+            pltpu.VMEM((16 * OVER, HD), half),
+            pltpu.VMEM((8, SLOT, width), half),
+            pltpu.VMEM((8, OVER, HD), half),
+            pltpu.VMEM((4, SLOT, width), half),
+            pltpu.VMEM((4, OVER, HD), half),
+            pltpu.VMEM((3, SLOT, width), half),
+            pltpu.VMEM((3, OVER, HD), half),
+            pltpu.VMEM((width, 2 * hid_dev), half),
+            pltpu.VMEM((hid_dev, width), half),
+            pltpu.VMEM((8, width), jnp.float32),
+            pltpu.VMEM((72, HD), jnp.float32),
+            pltpu.VMEM((5 * 272, hid_dev), half),
+            pltpu.VMEM((272, 2 * hid_dev), jnp.float32),
+            pltpu.VMEM((rows, quarter), jnp.float32),
+            pltpu.VMEM((EXPERTS * MAIN, quarter), half),
+            pltpu.VMEM((EXPERTS * TILE_ROWS, HD), half),
+            pltpu.VMEM((SLOT, width), half),
+            pltpu.VMEM((OVER, HD), half),
+            pltpu.VMEM((EXPERTS * MAIN, quarter), half),
+            pltpu.VMEM((EXPERTS * TILE_ROWS, HD), half),
+            pltpu.VMEM((16, width), half),
+            pltpu.VMEM((16, width), half),
+            pltpu.VMEM((36 * 16, 4 * OVER), half),
+            pltpu.VMEM((4 * OVER, 36 * 16), half),
+            pltpu.VMEM((4, 8, rows), jnp.float32),
+            dma((5,)),
+            dma((4,)),
+            dma((4,)),
+            dma((4,)),
+            dma((2,)),
+            dma((GROUP, 2)),
+            dma((4, 2)),
+            dma((4, 2)),
+            dma((3, 2)),
+            dma((3, 2)),
+            dma((8, 2)),
+            dma((8, 2)),
+            dma((8, 2)),
+            dma((8, 2)),
+            dma((4, 2)),
+            dma((4, 2)),
+            dma((3, 2)),
+            dma((3, 2)),
+            dma((2,)),
+            dma((GROUP, 2)),
+        ],
+        compiler_params=pltpu.CompilerParams(
+            collective_id=1, has_side_effects=True, vmem_limit_bytes=60 * 1024 * 1024
+        ),
+        cost_estimate=pl.CostEstimate(
+            flops=6 * 1088 * width * hid_dev, bytes_accessed=12 * 10**6, transcendentals=10**6
+        ),
+    )(
+        residual,
+        attended,
+        norm_gain.reshape(1, quarter),
+        routes,
+        routes.T,
+        route_weight,
+        w_gate,
+        gate_swapped,
+        w_up,
+        w_down,
+        wide,
+        tall,
+    )
 
 
 def local(
@@ -208,66 +854,20 @@
     scale_hidden,
     scale_out,
 ):
-    tok_rows = queries.shape[0]
-    n_dp = lax.axis_size("dp")
-    n_tensor = lax.axis_size("tensor")
-    attended = attend(queries, keys, values)
-    hidden_state = residual.astype(jnp.float32) + attended.astype(
-        jnp.float32
-    )
-    square_total = lax.psum(jnp.sum(hidden_state * hidden_state, axis=1), "tensor")
-    inverse = lax.rsqrt(square_total / D + EPS)
-    normed = (hidden_state * inverse[:, None] * norm_gain[None, :]).astype(jnp.bfloat16)
-    flat_routes = routes.reshape(-1)
-    route_rows = flat_routes.shape[0]
-    member = (flat_routes[:, None] == jnp.arange(EXPERTS, dtype=jnp.int32)[None, :]).astype(
-        jnp.int32
-    )
-    ranks = jnp.sum((jnp.cumsum(member, axis=0) - member) * member, axis=1)
-    slot_index = flat_routes * CAP + ranks
-    slot_hit = (slot_index[:, None] == jnp.arange(EXPERTS * CAP, dtype=jnp.int32)[None, :]).astype(
-        jnp.float32
-    )
-    token_hit = (
-        (jnp.arange(route_rows, dtype=jnp.int32) // TOP)[:, None]
-        == jnp.arange(tok_rows, dtype=jnp.int32)[None, :]
-    ).astype(jnp.float32)
-    dispatch = jnp.dot(slot_hit.T, token_hit, precision=lax.Precision.HIGHEST).astype(jnp.bfloat16)
-    combine = jnp.dot(
-        token_hit.T, slot_hit * route_weight.reshape(-1)[:, None], precision=lax.Precision.HIGHEST
-    )
-    tensor_pos = lax.axis_index("tensor")
-    widened = lax.all_gather(normed, "tensor", axis=1, tiled=True)
-    own_slots = lax.dynamic_index_in_dim(
-        dispatch.reshape(n_dp, n_tensor, CAP, tok_rows), tensor_pos, axis=1, keepdims=False
-    ).reshape(n_dp * CAP, tok_rows)
-    outgoing = jnp.dot(own_slots, widened, preferred_element_type=jnp.float32).astype(jnp.bfloat16)
-    expert_rows = lax.all_to_all(outgoing, "dp", split_axis=0, concat_axis=0, tiled=True)
-    activated = activate(
-        lax.all_gather(expert_rows, "context", axis=0, tiled=True),
+    attended, gate_swapped = attend(queries, keys, values, w_gate[0])
+    return experts(
+        residual,
+        attended,
+        norm_gain,
+        routes,
+        route_weight,
+        gate_swapped,
         w_gate[0],
         w_up[0],
-        scale_hidden[0, 0][None, :],
-        scale_hidden[0, 1][None, :],
+        w_down[0],
+        scale_hidden[0],
+        scale_out,
     )
-    summed = lax.psum_scatter(
-        jnp.dot(activated, w_down[0], preferred_element_type=jnp.float32).astype(jnp.bfloat16),
-        "context",
-        scatter_dimension=0,
-        tiled=True,
-    ).astype(jnp.float32)
-    expert_out = (summed * scale_out[0][None, :]).astype(jnp.bfloat16)
-    returned = lax.all_to_all(expert_out, "dp", split_axis=0, concat_axis=0, tiled=True)
-    own_combine = lax.dynamic_index_in_dim(
-        combine.reshape(tok_rows, n_dp, n_tensor, CAP), tensor_pos, axis=2, keepdims=False
-    ).reshape(tok_rows, n_dp * CAP)
-    partial_full = jnp.dot(
-        own_combine, returned.astype(jnp.float32), precision=lax.Precision.HIGHEST
-    )
-    routed = lax.psum_scatter(
-        partial_full.astype(jnp.bfloat16), "tensor", scatter_dimension=1, tiled=True
-    ).astype(jnp.float32)
-    return (hidden_state + routed).astype(jnp.bfloat16)
 
 
 def solution(mesh):

time: 498 us -> 310 us (0.62)
  Pallas kernels: 44 us -> 291 us
  waiting for transfers between devices: 176 us -> 0 us
  blocking collectives: 152 us -> 0 us
  local copies, waits for them, and re-layouts: 56.2 us -> 12.5 us
  matrix products: 34.6 us -> 0 us
  between operations: 13.9 us -> 0.05 us
  other arithmetic: 12.8 us -> 1.38 us
  starting transfers between devices: 6.69 us -> 0 us
    pallas_call x1 -> x2, Pallas kernels: 44 us -> 291 us  [the longest x1 224 us: experts(): pl.pallas_call(expert_kernel, out_shape=jax.ShapeDtypeStruct((rows, quart...]
    all_gather x2 -> x0, waiting for transfers between devices: 133 us -> none  [the longest x1 121 us: local(): lax.all_gather(expert_rows, 'context', axis=0, tiled=True)]
    unnamed x1 -> x0, blocking collectives: 123 us -> none
    unnamed x5 -> x0, waiting for transfers between devices: 35.4 us -> none
    dot_general x6 -> x0, matrix products: 34.6 us -> none  [the longest x1 16.8 us: local(): jnp.dot(activated, w_down[0], preferred_element_type=jnp.float32)]
    unnamed x35 -> x13, local copies, waits for them, and re-layouts: 35.9 us -> 9.86 us
    all_to_all x1 -> x0, blocking collectives: 18.6 us -> none  [local(): lax.all_to_all(outgoing, 'dp', split_axis=0, concat_axis=0, tiled=True)]
    psum x1 -> x0, blocking collectives: 11.1 us -> none  [local(): lax.psum(jnp.sum(hidden_state * hidden_state, axis=1), 'tensor')]
  transfers between devices with their start and end apart: 5 -> 0, of which waited for: 5 -> 0; matrix products, arithmetic and copies ran while one was open for 5% -> 0% of each run, Pallas kernels for 0% -> 0%
where the time goes in v2:
time: 310 us; the launch traced here: 305 us
  Pallas kernels  291 us (94%)
  local copies, waits for them, and re-layouts  12.5 us (4%)
    pallas_call x1, Pallas kernels, experts(): pl.pallas_call(expert_kernel, out_shape=jax.ShapeDtypeStruct((rows, quart...  224 us
    pallas_call x1, Pallas kernels, attend(): pl.pallas_call(attention_kernel, out_shape=(jax.ShapeDtypeStruct((rows, w...  67.1 us
    unnamed x13, local copies, waits for them, and re-layouts  9.86 us

profile of v2, /device:TPU:8, one launch (start us, length us, event | category | flops | bytes accessed | tf_op | source)
XLA Modules:
  0.0 304.7 jit_solution(17485040112276048725)
XLA Ops:
  0.0 0.7 reshape_squeeze.3
  0.7 1.3 reshape.9.gain_ref
  2.0 0.8 reduce
  2.8 0.6 select_maximum_fusion.tall_own
  3.4 1.4 copy.16.weight_ref
  4.8 1.4 copy.15.routes_ref
  6.2 0.7 broadcast_in_dim.8.wide_own
  6.9 0.0 copy-start
  6.9 1.0 copy-done
  7.8 0.0 copy-start.1
  7.8 1.0 copy-done.1
  8.8 0.0 copy-start.2
  8.8 1.0 copy-done.2
  9.8 67.1 %shard_map.118 = (bf16[128,1152]{1,0:T(8,128)(2,1)S(1)}, bf16[4608,384]{1,0:T(8,128)(2,1)S(1)}) custom-call(bf16[128,1152]{1,0:T(8,128)(2,1)S(1)} %copy-done, bf16[128,1152]{1,0:T(8,128)(2,1)S(1)} %copy-done.1, bf16[128,1152]{1,0:T(8,128)(2,1)S(1)} %copy-done.2, bf16[4608,384]{1,0:T(8,128)(2,1)} %bitcast.5), custom_call_target="tpu_custom_call" | custom-call | flops 1073741824 | bytes 1000000 | tf_op jit(solution)/shard_map/pallas_call | solution.py:196
  76.8 0.0 copy-start.3
  76.9 1.7 copy-done.3
  78.6 0.0 copy-start.4
  78.6 0.7 copy-done.4
  79.3 223.7 %shard_map.119 = bf16[128,1152]{1,0:T(8,128)(2,1)} custom-call(bf16[128,1152]{1,0:T(8,128)(2,1)} %residual_ref.1, bf16[128,1152]{1,0:T(8,128)(2,1)} %copy-done.4, f32[1,1152]{1,0:T(1,128)} %reshape.9.gain_ref, s32[128,2]{1,0:T(8,128)} %copy.15.routes_ref, s32[2,128]{1,0:T(2,128)} %bitcast.8, f32[128,2]{1,0:T(8,128)} %copy.16.weight_ref, ...), custom_call_target="tpu_custom_call" | custom-call | flops 11551113216 | bytes 12000000 | tf_op jit(solution)/shard_map/pallas_call | solution.py:766
  303.0 1.7 copy.18
  (2 shorter events, 0.0 us)
Async XLA Ops:
  6.9 1.0 copy-start
  7.8 1.0 copy-start.1
  8.8 1.0 copy-start.2
  76.8 1.7 copy-start.3
  78.6 0.7 copy-start.4

commit v3 on v2

--- a/solution.py
+++ b/solution.py
@@ -12,6 +12,9 @@
 EXPERTS = 16
 EPS = 1e-06
 NEG = -1e30
+PIECES = 12
+IN_FLIGHT = 2
+EARLY = 8
 N_CTX = 16
 HEADS_HERE = 9
 MESH = pl.DeviceIdType.MESH
@@ -57,14 +60,27 @@
 
     pl.semaphore_signal(barrier, inc=1, device_id=diagonal, device_id_type=MESH)
     pl.semaphore_wait(barrier, N_CTX)
-    swap = pltpu.make_async_remote_copy(
-        src_ref=gate_ref,
-        dst_ref=gate_out,
-        send_sem=gate_send,
-        recv_sem=gate_recv,
-        device_id=diagonal,
-        device_id_type=MESH,
-    )
+    depth = gate_ref.shape[0] // PIECES
+
+    def piece(number):
+        part = pl.ds(pl.multiple_of(number * depth, depth), depth)
+        return pltpu.make_async_remote_copy(
+            src_ref=gate_ref.at[part, :],
+            dst_ref=gate_out.at[part, :],
+            send_sem=gate_send.at[number],
+            recv_sem=gate_recv,
+            device_id=diagonal,
+            device_id_type=MESH,
+        )
+
+    def pump(first, count):
+        @pl.when(swapping)
+        def _():
+            @pl.loop(first, first + count)
+            def _(number):
+                piece(number - IN_FLIGHT).wait_send()
+                piece(number).start()
+
 
     my_rows = pl.ds(pl.multiple_of(ctx * rows, rows), rows)
     sources = (k_ref, q_ref, v_ref)
@@ -105,7 +121,8 @@
 
     @pl.when(swapping)
     def _():
-        swap.start()
+        for number in range(IN_FLIGHT):
+            piece(number).start()
 
     base = lax.rem(ctx + 8 * core, N_CTX)
     my_head = lax.div(base * HEADS_HERE + N_CTX - 1, N_CTX)
@@ -138,6 +155,8 @@
             @pl.when(ctx == block)
             def _():
                 pltpu.make_async_copy(src, dst, out_recv).start()
+
+    pump(2, 2)
 
     @pl.when(active)
     def _():
@@ -173,6 +192,13 @@
             ob[low:high, :] = (result / total).astype(jnp.bfloat16)
             give(2 * number + 1, True)
             give(2 * number, True)
+            if number in (6, 4):
+                pump(4 + (6 - number) // 2, 1)
+        pump(6, 2)
+
+    @pl.when(jnp.logical_not(active))
+    def _():
+        pump(4, 4)
 
     @pl.loop(0, HEADS_HERE)
     def _(step):
@@ -187,7 +213,10 @@
 
     @pl.when(swapping)
     def _():
-        swap.wait()
+        for number in range(EARLY - IN_FLIGHT, EARLY):
+            piece(number).wait_send()
+        landed = gate_out.at[pl.ds(0, EARLY * depth), :]
+        pltpu.make_async_copy(landed, landed, gate_recv).wait()
 
 
 def attend(queries, keys, values, w_gate):
@@ -210,7 +239,7 @@
             pltpu.SemaphoreType.DMA((HEADS_HERE, 3)),
             pltpu.SemaphoreType.DMA((N_CTX,)),
             pltpu.SemaphoreType.DMA,
-            pltpu.SemaphoreType.DMA,
+            pltpu.SemaphoreType.DMA((EARLY,)),
             pltpu.SemaphoreType.DMA,
         ],
         compiler_params=pltpu.CompilerParams(
@@ -328,6 +357,7 @@
     rsb_send,
     ret_recv,
     ret_send,
+    piece_send,
 ):
     dp, ctx, tensor = lax.axis_index("dp"), lax.axis_index("context"), lax.axis_index("tensor")
     core, y_hi = lax.rem(dp, 2), lax.div(dp, 2)
@@ -380,8 +410,19 @@
 
     swapping = core != y_lo
     up_part = w1.at[:, pl.ds(hid_dev, hid_dev)]
-    gate_part = w1.at[:, pl.ds(0, hid_dev)]
-    moved = ((up_own, up_part), (down_own, wd), (wide_own, wide), (tall_own, tall))
+    half_width = width // 2
+    early_part = w1.at[pl.ds(0, EARLY * (width // PIECES)), pl.ds(0, hid_dev)]
+    late_part = w1.at[pl.ds(EARLY * (width // PIECES), (PIECES - EARLY) * (width // PIECES)), pl.ds(0, hid_dev)]
+    down_half = [wd.at[:, pl.ds(half * half_width, half_width)] for half in range(2)]
+    moved = (
+        (up_own, up_part),
+        (down_own.at[:, pl.ds(0, half_width)], down_half[0]),
+        (wide_own, wide),
+        (tall_own, tall),
+        (gate_own.at[pl.ds(0, EARLY * (width // PIECES)), :], early_part),
+        (gate_own.at[pl.ds(EARLY * (width // PIECES), (PIECES - EARLY) * (width // PIECES)), :], late_part),
+        (down_own.at[:, pl.ds(half_width, half_width)], down_half[1]),
+    )
 
     def swap(index):
         return pltpu.make_async_remote_copy(
@@ -393,18 +434,60 @@
             device_id_type=MESH,
         )
 
+    early_rows = EARLY * (width // PIECES)
+    n_gate = PIECES - EARLY
+    n_pieces = n_gate + 2 * PIECES
+
+    def load(number):
+        if number < n_gate + PIECES:
+            depth = width // PIECES
+            gate_piece = number < n_gate
+            start = (EARLY + number if gate_piece else number - n_gate) * depth
+            part = pl.ds(start, depth)
+            src = (gate_own if gate_piece else up_own).at[part, :]
+            dst = w1.at[part, pl.ds(0 if gate_piece else hid_dev, hid_dev)]
+            recv_sem = w_recv.at[5 if gate_piece else 0]
+        else:
+            depth = width // PIECES
+            part = pl.ds((number - n_gate - PIECES) * depth, depth)
+            src, dst = down_own.at[:, part], wd.at[:, part]
+            recv_sem = w_recv.at[1 if number < n_gate + PIECES + PIECES // 2 else 6]
+        return pltpu.make_async_remote_copy(
+            src_ref=src,
+            dst_ref=dst,
+            send_sem=piece_send.at[number],
+            recv_sem=recv_sem,
+            device_id=diagonal,
+            device_id_type=MESH,
+        )
+
+    progress = [0]
+
+    def pump(count):
+        first = progress[0]
+        progress[0] = min(first + count, n_pieces)
+
+        @pl.when(swapping)
+        def _():
+            for number in range(first, progress[0]):
+                if number >= IN_FLIGHT:
+                    load(number - IN_FLIGHT).wait_send()
+                load(number).start()
+
     @pl.when(swapping)
     def _():
-        for index in (2, 3, 0, 1):
+        for index in (2, 3):
             swap(index).start()
-        pltpu.make_async_copy(gate_swapped, gate_part, w_recv.at[4]).start()
+        pltpu.make_async_copy(
+            gate_swapped.at[pl.ds(0, early_rows), :], early_part, w_recv.at[4]
+        ).start()
 
     @pl.when(jnp.logical_not(swapping))
     def _():
-        for index in (2, 3, 0, 1):
+        for index in range(7):
             pltpu.make_async_copy(moved[index][0], moved[index][1], w_recv.at[index]).start()
-        pltpu.make_async_copy(gate_own, gate_part, w_recv.at[4]).start()
-
+
+    pump(IN_FLIGHT)
     state = residual_ref[...].astype(jnp.float32) + attended_ref[...].astype(jnp.float32)
     hidden[...] = state
     own_squares = jnp.sum(state * state, axis=1, keepdims=True)
@@ -516,12 +599,14 @@
     def share(slot):
         pass_on(slot, twin(slot), sibx_send, sibx_recv, CARRIED.index(slot), sibling)
 
+    pump(3)
     arrived(xm.at[main(OWN), :], disp_recv.at[0])
     arrived(xo.at[over(OWN), :], disp_recv.at[1])
     pass_on(OWN, major(1), aga_send, aga_recv, 0, ahead)
     pass_on(OWN, minor(1), agb_send, agb_recv, 0, behind)
     share(OWN)
     for k in (1, 2, 3):
+        pump(4)
         landed(major(k), aga_recv, k - 1)
         pass_on(major(k), major(k + 1), aga_send, aga_recv, k, ahead)
         share(major(k))
@@ -561,145 +646,226 @@
                 gate / (1.0 + jnp.exp(-gate)) * up
             ).astype(jnp.bfloat16)
 
-    def down_part(step):
+    def lanes_of(half, n):
+        start = half * half_width + n * 768
+        return pl.ds(start if isinstance(n, int) else pl.multiple_of(start, 256), 768)
+
+    def down_part(step, half):
         low, count = STEPS[step]
         size = step_rows(step)
 
-        @pl.loop(0, width // 512)
+        @pl.loop(0, half_width // 768)
         def _(n):
-            lanes = pl.ds(pl.multiple_of(n * 512, 512), 512)
+            lanes = lanes_of(half, n)
             result = exact_dot(act[step * 272 : step * 272 + size + 16, :], wd[:, lanes])
             result = result.astype(jnp.bfloat16)
             ym[low * SLOT : low * SLOT + size, lanes] = result[0:size, :]
-            over_y[:, lanes] = result[size:, :]
-
-        stack = jnp.concatenate([over_y[:, n * HD : (n + 1) * HD] for n in range(36)], axis=0)
-        yo[low * OVER : (low + count) * OVER, :] = exact_dot(
-            gather[0 : count * OVER, :], stack
-        ).astype(jnp.bfloat16)
+            over_y[step * 16 : step * 16 + 16, lanes] = result[size:, :]
+
+        if half:
+            stack = jnp.concatenate(
+                [over_y[step * 16 : step * 16 + 16, n * HD : (n + 1) * HD] for n in range(36)], axis=0
+            )
+            yo[low * OVER : (low + count) * OVER, :] = exact_dot(
+                gather[0 : count * OVER, :], stack
+            ).astype(jnp.bfloat16)
+        part = pl.ds(half * half_width, half_width)
         for slot in CARRIED:
             if low <= slot < low + count:
                 number = CARRIED.index(slot)
                 other = twin(slot)
-                send(ym.at[main(other), :], sib_m.at[number], siby_send.at[number, 0], siby_recv.at[number, 0], sibling)
-                send(yo.at[over(other), :], sib_o.at[number], siby_send.at[number, 1], siby_recv.at[number, 1], sibling)
-
-    arrived(gate_part, w_recv.at[4])
+                send(
+                    ym.at[main(other), part],
+                    sib_m.at[number, :, part],
+                    siby_send.at[number, half],
+                    siby_recv.at[number, half],
+                    sibling,
+                )
+                if half:
+                    send(
+                        yo.at[over(other), :],
+                        sib_o.at[number],
+                        siby_send.at[number, 2],
+                        siby_recv.at[number, 2],
+                        sibling,
+                    )
+
+    pump(3)
+    arrived(early_part, w_recv.at[4])
+    arrived(late_part, w_recv.at[5])
     arrived(up_part, w_recv.at[0])
     arrived(wide, w_recv.at[2])
     arrived(tall, w_recv.at[3])
     for step in (0, 1, 2, 3):
         fetch_shared(step)
         hidden_part(step)
+        pump(1)
     landed(major(4), aga_recv, 3)
     share(major(4))
     fetch_shared(4)
     hidden_part(4)
-    arrived(wd, w_recv.at[1])
-
-    def add_up(slot, extras):
+    pump(max(0, n_gate + PIECES + PIECES // 2 - progress[0]))
+    arrived(down_half[0], w_recv.at[1])
+
+    def summed(own, others):
+        value = own.astype(jnp.float32)
+        for other in others:
+            value = value + other.astype(jnp.float32)
+        return value
+
+    def await_parts(slot, extras, half):
         number = CARRIED.index(slot)
-        arrived(sib_m.at[number], siby_recv.at[number, 0])
-        arrived(sib_o.at[number], siby_recv.at[number, 1])
-
-        def summed(own, others):
-            value = own.astype(jnp.float32)
-            for other in others:
-                value = value + other.astype(jnp.float32)
-            return value
-
-        def block(lanes):
-            return summed(
-                ym[main(slot), lanes],
-                [sib_m[number, :, lanes]] + [ref[place, :, lanes] for ref, _, place in extras],
+        part = pl.ds(half * half_width, half_width)
+        arrived(sib_m.at[number, :, part], siby_recv.at[number, half])
+        for ref_m, ref_o, spot, sems in extras:
+            arrived(ref_m.at[spot, :, part], sems.at[spot, half])
+        if half:
+            arrived(sib_o.at[number], siby_recv.at[number, 2])
+            for ref_m, ref_o, spot, sems in extras:
+                arrived(ref_o.at[spot], sems.at[spot, 2])
+
+    def block(slot, extras, lanes):
+        number = CARRIED.index(slot)
+        return summed(
+            ym[main(slot), lanes],
+            [sib_m[number, :, lanes]] + [extra[0][extra[2], :, lanes] for extra in extras],
+        )
+
+    def tiles(slot, extras):
+        number = CARRIED.index(slot)
+        return summed(yo[over(slot), :], [sib_o[number]] + [extra[1][extra[2]] for extra in extras])
+
+    def hop(slot, extras, half, goal_m, goal_o, send_sem, recv_sem, number, device):
+        await_parts(slot, extras, half)
+
+        @pl.loop(0, half_width // 768)
+        def _(n):
+            lanes = lanes_of(half, n)
+            ym[main(slot), lanes] = block(slot, extras, lanes).astype(jnp.bfloat16)
+
+        part = pl.ds(half * half_width, half_width)
+        send(
+            ym.at[main(slot), part],
+            goal_m.at[number, :, part],
+            send_sem.at[number, half],
+            recv_sem.at[number, half],
+            device,
+        )
+        if half:
+            yo[over(slot), :] = tiles(slot, extras).astype(jnp.bfloat16)
+            send(
+                yo.at[over(slot), :],
+                goal_o.at[number],
+                send_sem.at[number, 2],
+                recv_sem.at[number, 2],
+                device,
             )
 
-        tiles = summed(
-            yo[over(slot), :], [sib_o[number]] + [ref[place] for _, ref, place in extras]
-        )
-        return block, tiles
-
-    def hop(slot, extras, goal_m, goal_o, send_sem, recv_sem, number, device):
-        for ref_m, ref_o, place, sems in extras:
-            arrived(ref_m.at[place], sems.at[place, 0])
-            arrived(ref_o.at[place], sems.at[place, 1])
-        block, tiles = add_up(slot, [e[:3] for e in extras])
-
-        @pl.loop(0, width // 512)
+    def hop_a(k, half):
+        extras = [(rxa_m, rxa_o, k, rsa_recv)] if k < 4 else []
+        hop(major(k), extras, half, rxa_m, rxa_o, rsa_send, rsa_recv, k - 1, behind)
+
+    def hop_b(k, half):
+        extras = [(rxb_m, rxb_o, k, rsb_recv)] if k < 3 else []
+        hop(minor(k), extras, half, rxb_m, rxb_o, rsb_send, rsb_recv, k - 1, ahead)
+
+    def give_back(step, half):
+        spot = lax.rem(place + lax.div(step, 2), 4)
+        part = 2 * half + lax.rem(tensor + step, 2)
+        other = spot * 4 + part
+        return other, eo_m.at[rows_of(spot), columns_of(part)], ret_m.at[rows_of(rank), :]
+
+    def give_all(half, start):
+        @pl.loop(0, 8)
+        def _(step):
+            other, src, dst = give_back(step, half)
+
+            @pl.when(other != rank)
+            def _():
+                copy = pltpu.make_async_remote_copy(
+                    src_ref=src,
+                    dst_ref=dst,
+                    send_sem=ret_send.at[half * 8 + step, 0],
+                    recv_sem=ret_recv.at[0],
+                    device_id=member(other),
+                    device_id_type=MESH,
+                )
+                if start:
+                    copy.start()
+                else:
+                    copy.wait_send()
+
+            if start:
+
+                @pl.when(other == rank)
+                def _():
+                    pltpu.make_async_copy(src, dst, ret_recv.at[0]).start()
+
+    def give_over(step):
+        other = lax.rem(rank + step, GROUP)
+        return pltpu.make_async_remote_copy(
+            src_ref=eo_o.at[rows_of(other), :],
+            dst_ref=ret_o.at[rows_of(rank), :],
+            send_sem=ret_send.at[step, 1],
+            recv_sem=ret_recv.at[1],
+            device_id=member(other),
+            device_id_type=MESH,
+        )
+
+    def finish(half):
+        last = [(rxb_m, rxb_o, 0, rsb_recv), (rxa_m, rxa_o, 0, rsa_recv)]
+        await_parts(OWN, last, half)
+
+        @pl.loop(0, half_width // 768)
         def _(n):
-            lanes = pl.ds(pl.multiple_of(n * 512, 512), 512)
-            ym[main(slot), lanes] = block(lanes).astype(jnp.bfloat16)
-
-        send(ym.at[main(slot), :], goal_m.at[number], send_sem.at[number, 0], recv_sem.at[number, 0], device)
-        yo[over(slot), :] = tiles.astype(jnp.bfloat16)
-        send(yo.at[over(slot), :], goal_o.at[number], send_sem.at[number, 1], recv_sem.at[number, 1], device)
-
-    def hop_a(k):
-        extras = [(rxa_m, rxa_o, k, rsa_recv)] if k < 4 else []
-        hop(major(k), extras, rxa_m, rxa_o, rsa_send, rsa_recv, k - 1, behind)
-
-    def hop_b(k):
-        extras = [(rxb_m, rxb_o, k, rsb_recv)] if k < 3 else []
-        hop(minor(k), extras, rxb_m, rxb_o, rsb_send, rsb_recv, k - 1, ahead)
-
-    down_part(4)
-    hop_a(4)
-    down_part(3)
-    hop_b(3)
-    down_part(2)
-    down_part(1)
-    down_part(0)
-    hop_a(3)
-    hop_b(2)
-    hop_a(2)
-    hop_b(1)
-    hop_a(1)
-    last = [(rxb_m, rxb_o, 0, rsb_recv), (rxa_m, rxa_o, 0, rsa_recv)]
-    for ref_m, ref_o, spot, sems in last:
-        arrived(ref_m.at[spot], sems.at[spot, 0])
-        arrived(ref_o.at[spot], sems.at[spot, 1])
-    block, tiles = add_up(OWN, [e[:3] for e in last])
-
-    @pl.loop(0, width // 512)
-    def _(n):
-        lanes = pl.ds(pl.multiple_of(n * 512, 512), 512)
-        eo_m[:, lanes] = (block(lanes) * wide[0:1, lanes]).astype(jnp.bfloat16)
-
-    for n in range(4):
-        eo_o[n * 64 : (n + 1) * 64, :] = (tiles[n * 64 : (n + 1) * 64, :] * tall[8:72, :]).astype(
-            jnp.bfloat16
-        )
-
-    def give_back(step):
-        other = lax.rem(rank + step, GROUP)
-        to_place, to_part = lax.div(other, 4), lax.rem(other, 4)
-        pairs = (
-            (eo_m.at[rows_of(to_place), columns_of(to_part)], ret_m.at[rows_of(rank), :]),
-            (eo_o.at[rows_of(other), :], ret_o.at[rows_of(rank), :]),
-        )
-        return [
-            pltpu.make_async_remote_copy(
-                src_ref=src,
-                dst_ref=dst,
-                send_sem=ret_send.at[step, index],
-                recv_sem=ret_recv.at[index],
-                device_id=member(other),
-                device_id_type=MESH,
-            )
-            for index, (src, dst) in enumerate(pairs)
-        ]
-
-    pltpu.make_async_copy(
-        eo_m.at[rows_of(place), columns_of(tensor)], ret_m.at[rows_of(rank), :], ret_recv.at[0]
-    ).start()
-    pltpu.make_async_copy(
-        eo_o.at[rows_of(rank), :], ret_o.at[rows_of(rank), :], ret_recv.at[1]
-    ).start()
-
-    @pl.loop(1, GROUP)
-    def _(step):
-        for copy in give_back(step):
-            copy.start()
+            lanes = lanes_of(half, n)
+            eo_m[:, lanes] = (block(OWN, last, lanes) * wide[0:1, lanes]).astype(jnp.bfloat16)
+
+        if half:
+            value = tiles(OWN, last)
+            for n in range(4):
+                eo_o[n * 64 : (n + 1) * 64, :] = (
+                    value[n * 64 : (n + 1) * 64, :] * tall[8:72, :]
+                ).astype(jnp.bfloat16)
+        give_all(half, True)
+        if half:
+            pltpu.make_async_copy(
+                eo_o.at[rows_of(rank), :], ret_o.at[rows_of(rank), :], ret_recv.at[1]
+            ).start()
+
+            @pl.loop(1, GROUP)
+            def _(step):
+                give_over(step).start()
+
+    down_part(4, 0)
+    hop_a(4, 0)
+    down_part(3, 0)
+    hop_b(3, 0)
+    for step in (2, 1, 0):
+        pump(1)
+        down_part(step, 0)
+    hop_a(3, 0)
+    hop_b(2, 0)
+    pump(1)
+    hop_a(2, 0)
+    hop_b(1, 0)
+    pump(n_pieces)
+    arrived(down_half[1], w_recv.at[6])
+    down_part(4, 1)
+    hop_a(4, 1)
+    down_part(3, 1)
+    hop_b(3, 1)
+    hop_a(1, 0)
+    down_part(2, 1)
+    hop_a(3, 1)
+    hop_b(2, 1)
+    down_part(1, 1)
+    hop_a(2, 1)
+    hop_b(1, 1)
+    down_part(0, 1)
+    finish(0)
+    hop_a(1, 1)
+    finish(1)
 
     expert_id = iotas(rows, EXPERTS)[1]
     hits = [expert_id == routes_ref[:, k : k + 1] for k in range(2)]
@@ -736,13 +902,18 @@
 
     @pl.loop(1, GROUP)
     def _(step):
-        for copy in dispatch(step) + give_back(step):
+        for copy in dispatch(step) + [give_over(step)]:
             copy.wait_send()
+
+    for half in range(2):
+        give_all(half, False)
 
     @pl.when(swapping)
     def _():
-        for index in range(4):
+        for index in (2, 3):
             swap(index).wait_send()
+        for number in range(n_pieces - IN_FLIGHT, n_pieces):
+            load(number).wait_send()
 
 
 def experts(
@@ -793,11 +964,11 @@
             pltpu.VMEM((EXPERTS * MAIN, quarter), half),
             pltpu.VMEM((EXPERTS * TILE_ROWS, HD), half),
             pltpu.VMEM((16, width), half),
-            pltpu.VMEM((16, width), half),
+            pltpu.VMEM((80, width), half),
             pltpu.VMEM((36 * 16, 4 * OVER), half),
             pltpu.VMEM((4 * OVER, 36 * 16), half),
             pltpu.VMEM((4, 8, rows), jnp.float32),
-            dma((5,)),
+            dma((7,)),
             dma((4,)),
             dma((4,)),
             dma((4,)),
@@ -809,14 +980,15 @@
             dma((3, 2)),
             dma((8, 2)),
             dma((8, 2)),
-            dma((8, 2)),
-            dma((8, 2)),
-            dma((4, 2)),
-            dma((4, 2)),
-            dma((3, 2)),
-            dma((3, 2)),
+            dma((8, 3)),
+            dma((8, 3)),
+            dma((4, 3)),
+            dma((4, 3)),
+            dma((3, 3)),
+            dma((3, 3)),
             dma((2,)),
             dma((GROUP, 2)),
+            dma((3 * PIECES - EARLY,)),
         ],
         compiler_params=pltpu.CompilerParams(
             collective_id=1, has_side_effects=True, vmem_limit_bytes=60 * 1024 * 1024

time: 310 us -> 235 us (0.76)
  Pallas kernels: 291 us -> 218 us
    pallas_call x1, Pallas kernels: 224 us -> 163 us  [experts(): pl.pallas_call(expert_kernel, out_shape=jax.ShapeDtypeStruct((rows, quart...]
    pallas_call x1, Pallas kernels: 67.1 us -> 54.8 us  [attend(): pl.pallas_call(attention_kernel, out_shape=(jax.ShapeDtypeStruct((rows, w...]
where the time goes in v3:
time: 235 us; the launch traced here: 232 us
  Pallas kernels  218 us (93%)
  local copies, waits for them, and re-layouts  12.5 us (5%)
    pallas_call x1, Pallas kernels, experts(): pl.pallas_call(expert_kernel, out_shape=jax.ShapeDtypeStruct((rows, quart...  163 us
    pallas_call x1, Pallas kernels, attend(): pl.pallas_call(attention_kernel, out_shape=(jax.ShapeDtypeStruct((rows, w...  54.8 us
    unnamed x13, local copies, waits for them, and re-layouts  9.86 us

profile of v3, /device:TPU:8, one launch (start us, length us, event | category | flops | bytes accessed | tf_op | source)
XLA Modules:
  0.0 231.7 jit_solution(7841751825358461652)
XLA Ops:
  0.0 0.7 reshape_squeeze.3
  0.7 1.3 reshape.9.gain_ref
  2.0 0.8 reduce
  2.8 0.6 select_maximum_fusion.tall_own
  3.4 1.4 copy.16.weight_ref
  4.8 1.4 copy.15.routes_ref
  6.2 0.7 broadcast_in_dim.8.wide_own
  6.9 0.0 copy-start
  6.9 1.0 copy-done
  7.8 0.0 copy-start.1
  7.8 1.0 copy-done.1
  8.8 0.0 copy-start.2
  8.8 1.0 copy-done.2
  9.8 54.8 %shard_map.118 = (bf16[128,1152]{1,0:T(8,128)(2,1)S(1)}, bf16[4608,384]{1,0:T(8,128)(2,1)S(1)}) custom-call(bf16[128,1152]{1,0:T(8,128)(2,1)S(1)} %copy-done, bf16[128,1152]{1,0:T(8,128)(2,1)S(1)} %copy-done.1, bf16[128,1152]{1,0:T(8,128)(2,1)S(1)} %copy-done.2, bf16[4608,384]{1,0:T(8,128)(2,1)} %bitcast.5), custom_call_target="tpu_custom_call" | custom-call | flops 1073741824 | bytes 1000000 | tf_op jit(solution)/shard_map/pallas_call | solution.py:225
  64.6 0.0 copy-start.3
  64.6 1.7 copy-done.3
  66.4 0.0 copy-start.4
  66.4 0.7 copy-done.4
  67.1 162.9 %shard_map.119 = bf16[128,1152]{1,0:T(8,128)(2,1)} custom-call(bf16[128,1152]{1,0:T(8,128)(2,1)} %residual_ref.1, bf16[128,1152]{1,0:T(8,128)(2,1)} %copy-done.4, f32[1,1152]{1,0:T(1,128)} %reshape.9.gain_ref, s32[128,2]{1,0:T(8,128)} %copy.15.routes_ref, s32[2,128]{1,0:T(2,128)} %bitcast.8, f32[128,2]{1,0:T(8,128)} %copy.16.weight_ref, ...), custom_call_target="tpu_custom_call" | custom-call | flops 11551113216 | bytes 12000000 | tf_op jit(solution)/shard_map/pallas_call | solution.py:937
  230.0 1.7 copy.18
  (2 shorter events, 0.0 us)
Async XLA Ops:
  6.9 1.0 copy-start
  7.8 1.0 copy-start.1
  8.8 1.0 copy-start.2
  64.6 1.7 copy-start.3
  66.4 0.7 copy-start.4

commit v4 on v3

--- a/solution.py
+++ b/solution.py
@@ -13,8 +13,8 @@
 EPS = 1e-06
 NEG = -1e30
 PIECES = 12
-IN_FLIGHT = 2
-EARLY = 8
+IN_FLIGHT = 3
+EARLY = 12
 N_CTX = 16
 HEADS_HERE = 9
 MESH = pl.DeviceIdType.MESH
@@ -25,63 +25,12 @@
     return lax.rem(lax.div(head * N_CTX, HEADS_HERE) + 8 * core, N_CTX)
 
 
-def attention_kernel(
-    q_ref,
-    k_ref,
-    v_ref,
-    gate_ref,
-    out_ref,
-    gate_out,
-    qs,
-    ks,
-    vs,
-    ob,
-    recv_sem,
-    send_sem,
-    out_send,
-    out_recv,
-    gate_send,
-    gate_recv,
+def attention_phase(
+    q_ref, k_ref, v_ref, out_ref, qs, ks, vs, ob, recv_sem, send_sem, out_send, out_recv, pump
 ):
     ctx = lax.axis_index("context")
-    dp = lax.axis_index("dp")
-    core = lax.rem(dp, 2)
-    swapping = core != lax.div(ctx, N_CTX // 2)
-    diagonal = {"dp": dp + 1 - 2 * core, "context": lax.rem(ctx + N_CTX // 2, N_CTX)}
+    core = lax.rem(lax.axis_index("dp"), 2)
     rows = q_ref.shape[0]
-
-    barrier = pltpu.get_barrier_semaphore()
-
-    @pl.loop(1, N_CTX)
-    def _(step):
-        pl.semaphore_signal(
-            barrier, inc=1, device_id={"context": lax.rem(ctx + step, N_CTX)}, device_id_type=MESH
-        )
-
-    pl.semaphore_signal(barrier, inc=1, device_id=diagonal, device_id_type=MESH)
-    pl.semaphore_wait(barrier, N_CTX)
-    depth = gate_ref.shape[0] // PIECES
-
-    def piece(number):
-        part = pl.ds(pl.multiple_of(number * depth, depth), depth)
-        return pltpu.make_async_remote_copy(
-            src_ref=gate_ref.at[part, :],
-            dst_ref=gate_out.at[part, :],
-            send_sem=gate_send.at[number],
-            recv_sem=gate_recv,
-            device_id=diagonal,
-            device_id_type=MESH,
-        )
-
-    def pump(first, count):
-        @pl.when(swapping)
-        def _():
-            @pl.loop(first, first + count)
-            def _(number):
-                piece(number - IN_FLIGHT).wait_send()
-                piece(number).start()
-
-
     my_rows = pl.ds(pl.multiple_of(ctx * rows, rows), rows)
     sources = (k_ref, q_ref, v_ref)
     targets = (ks, qs, vs)
@@ -119,10 +68,7 @@
     def _(step):
         scatter(step, True)
 
-    @pl.when(swapping)
-    def _():
-        for number in range(IN_FLIGHT):
-            piece(number).start()
+    pump(0, 4)
 
     base = lax.rem(ctx + 8 * core, N_CTX)
     my_head = lax.div(base * HEADS_HERE + N_CTX - 1, N_CTX)
@@ -155,8 +101,6 @@
             @pl.when(ctx == block)
             def _():
                 pltpu.make_async_copy(src, dst, out_recv).start()
-
-    pump(2, 2)
 
     @pl.when(active)
     def _():
@@ -194,11 +138,11 @@
             give(2 * number, True)
             if number in (6, 4):
                 pump(4 + (6 - number) // 2, 1)
-        pump(6, 2)
+        pump(6, EARLY - 6)
 
     @pl.when(jnp.logical_not(active))
     def _():
-        pump(4, 4)
+        pump(4, EARLY - 4)
 
     @pl.loop(0, HEADS_HERE)
     def _(step):
@@ -210,45 +154,6 @@
             give(block, False)
 
     pltpu.make_async_copy(out_ref, out_ref, out_recv).wait()
-
-    @pl.when(swapping)
-    def _():
-        for number in range(EARLY - IN_FLIGHT, EARLY):
-            piece(number).wait_send()
-        landed = gate_out.at[pl.ds(0, EARLY * depth), :]
-        pltpu.make_async_copy(landed, landed, gate_recv).wait()
-
-
-def attend(queries, keys, values, w_gate):
-    rows, width = queries.shape
-    length = rows * N_CTX
-    return pl.pallas_call(
-        attention_kernel,
-        out_shape=(
-            jax.ShapeDtypeStruct((rows, width), jnp.bfloat16),
-            jax.ShapeDtypeStruct(w_gate.shape, jnp.bfloat16),
-        ),
-        in_specs=[pl.BlockSpec(memory_space=pl.ANY)] * 4,
-        out_specs=(pl.BlockSpec(memory_space=pltpu.VMEM), pl.BlockSpec(memory_space=pl.ANY)),
-        scratch_shapes=[
-            pltpu.VMEM((length, HD), jnp.bfloat16),
-            pltpu.VMEM((length, HD), jnp.bfloat16),
-            pltpu.VMEM((length, HD), jnp.bfloat16),
-            pltpu.VMEM((length, HD), jnp.bfloat16),
-            pltpu.SemaphoreType.DMA((3,)),
-            pltpu.SemaphoreType.DMA((HEADS_HERE, 3)),
-            pltpu.SemaphoreType.DMA((N_CTX,)),
-            pltpu.SemaphoreType.DMA,
-            pltpu.SemaphoreType.DMA((EARLY,)),
-            pltpu.SemaphoreType.DMA,
-        ],
-        compiler_params=pltpu.CompilerParams(
-            collective_id=0, has_side_effects=True, vmem_limit_bytes=48 * 1024 * 1024
-        ),
-        cost_estimate=pl.CostEstimate(
-            flops=2 * length * length * HD, bytes_accessed=10**6, transcendentals=length * length // 2
-        ),
-    )(queries, keys, values, w_gate)
 
 
 MAIN = 16
@@ -295,20 +200,26 @@
     )
 
 
-def expert_kernel(
-    residual_ref,
-    attended_ref,
+def layer_kernel(
     gain_ref,
     routes_ref,
-    routes_t_ref,
     weight_ref,
-    gate_own,
-    gate_swapped,
-    up_own,
-    down_own,
+    residual_ref,
+    q_ref,
+    k_ref,
+    v_ref,
+    gate_all,
+    up_all,
+    down_all,
+    inner_all,
     wide_own,
-    tall_own,
     out_ref,
+    residual,
+    attended,
+    qs,
+    ks,
+    vs,
+    ob,
     xm,
     xo,
     ym,
@@ -322,6 +233,7 @@
     w1,
     wd,
     wide,
+    inner,
     tall,
     act,
     hid,
@@ -358,6 +270,11 @@
     ret_recv,
     ret_send,
     piece_send,
+    attn_recv,
+    attn_send,
+    out_send,
+    out_recv,
+    res_recv,
 ):
     dp, ctx, tensor = lax.axis_index("dp"), lax.axis_index("context"), lax.axis_index("tensor")
     core, y_hi = lax.rem(dp, 2), lax.div(dp, 2)
@@ -368,6 +285,9 @@
     rows, quarter = residual_ref.shape
     width = xm.shape[1]
     hid_dev = wd.shape[0]
+    gate_own, up_own, down_own, inner_own = (
+        ref.at[0] for ref in (gate_all, up_all, down_all, inner_all)
+    )
 
     def member(number):
         other = lax.div(number, 4)
@@ -392,7 +312,15 @@
             barrier, inc=1, device_id=member(lax.rem(rank + step, GROUP)), device_id_type=MESH
         )
 
-    pl.semaphore_wait(barrier, GROUP + 3)
+    @pl.loop(1, N_CTX)
+    def _(step):
+        pl.semaphore_signal(
+            barrier, inc=1, device_id={"context": lax.rem(ctx + step, N_CTX)}, device_id_type=MESH
+        )
+
+    load_residual = pltpu.make_async_copy(residual_ref, residual, res_recv)
+    load_residual.start()
+    pl.semaphore_wait(barrier, GROUP + N_CTX + 2)
 
     pending = []
 
@@ -409,19 +337,17 @@
         pending.append(copy)
 
     swapping = core != y_lo
+    gate_part = w1.at[:, pl.ds(0, hid_dev)]
     up_part = w1.at[:, pl.ds(hid_dev, hid_dev)]
     half_width = width // 2
-    early_part = w1.at[pl.ds(0, EARLY * (width // PIECES)), pl.ds(0, hid_dev)]
-    late_part = w1.at[pl.ds(EARLY * (width // PIECES), (PIECES - EARLY) * (width // PIECES)), pl.ds(0, hid_dev)]
     down_half = [wd.at[:, pl.ds(half * half_width, half_width)] for half in range(2)]
     moved = (
+        (gate_own, gate_part),
         (up_own, up_part),
         (down_own.at[:, pl.ds(0, half_width)], down_half[0]),
+        (down_own.at[:, pl.ds(half_width, half_width)], down_half[1]),
+        (inner_own, inner),
         (wide_own, wide),
-        (tall_own, tall),
-        (gate_own.at[pl.ds(0, EARLY * (width // PIECES)), :], early_part),
-        (gate_own.at[pl.ds(EARLY * (width // PIECES), (PIECES - EARLY) * (width // PIECES)), :], late_part),
-        (down_own.at[:, pl.ds(half_width, half_width)], down_half[1]),
     )
 
     def swap(index):
@@ -434,61 +360,61 @@
             device_id_type=MESH,
         )
 
-    early_rows = EARLY * (width // PIECES)
-    n_gate = PIECES - EARLY
-    n_pieces = n_gate + 2 * PIECES
+    n_pieces = 3 * PIECES
+    depth = width // PIECES
 
     def load(number):
-        if number < n_gate + PIECES:
-            depth = width // PIECES
-            gate_piece = number < n_gate
-            start = (EARLY + number if gate_piece else number - n_gate) * depth
-            part = pl.ds(start, depth)
-            src = (gate_own if gate_piece else up_own).at[part, :]
-            dst = w1.at[part, pl.ds(0 if gate_piece else hid_dev, hid_dev)]
-            recv_sem = w_recv.at[5 if gate_piece else 0]
+        which, part = number // PIECES, pl.ds(number % PIECES * depth, depth)
+        if which < 2:
+            src = (gate_own, up_own)[which].at[part, :]
+            dst = w1.at[part, pl.ds(which * hid_dev, hid_dev)]
         else:
-            depth = width // PIECES
-            part = pl.ds((number - n_gate - PIECES) * depth, depth)
             src, dst = down_own.at[:, part], wd.at[:, part]
-            recv_sem = w_recv.at[1 if number < n_gate + PIECES + PIECES // 2 else 6]
+            which += number % PIECES // (PIECES // 2)
         return pltpu.make_async_remote_copy(
             src_ref=src,
             dst_ref=dst,
             send_sem=piece_send.at[number],
-            recv_sem=recv_sem,
+            recv_sem=w_recv.at[which],
             device_id=diagonal,
             device_id_type=MESH,
         )
 
-    progress = [0]
-
-    def pump(count):
-        first = progress[0]
-        progress[0] = min(first + count, n_pieces)
-
+    def pump_at(first, count):
         @pl.when(swapping)
         def _():
-            for number in range(first, progress[0]):
+            for number in range(first, first + count):
                 if number >= IN_FLIGHT:
                     load(number - IN_FLIGHT).wait_send()
                 load(number).start()
 
+    progress = [EARLY]
+
+    def pump(count):
+        first = progress[0]
+        progress[0] = min(first + max(count, 0), n_pieces)
+        if progress[0] > first:
+            pump_at(first, progress[0] - first)
+
     @pl.when(swapping)
     def _():
-        for index in (2, 3):
+        for index in (4, 5):
             swap(index).start()
-        pltpu.make_async_copy(
-            gate_swapped.at[pl.ds(0, early_rows), :], early_part, w_recv.at[4]
-        ).start()
 
     @pl.when(jnp.logical_not(swapping))
     def _():
-        for index in range(7):
+        for index in range(6):
             pltpu.make_async_copy(moved[index][0], moved[index][1], w_recv.at[index]).start()
 
-    pump(IN_FLIGHT)
-    state = residual_ref[...].astype(jnp.float32) + attended_ref[...].astype(jnp.float32)
+    attention_phase(
+        q_ref, k_ref, v_ref, attended, qs, ks, vs, ob, attn_recv, attn_send, out_send, out_recv, pump_at
+    )
+    load_residual.wait()
+
+    def upright(line):
+        return jnp.broadcast_to(line, (rows, rows)).T[:, 0:1]
+
+    state = residual[...].astype(jnp.float32) + attended[...].astype(jnp.float32)
     hidden[...] = state
     own_squares = jnp.sum(state * state, axis=1, keepdims=True)
     squares[tensor] = jnp.broadcast_to(own_squares, (rows, rows)).T[0:8, :]
@@ -507,8 +433,9 @@
     for step in (1, 2, 3):
         tell(step).start()
 
+    pump(1)
     row, col = iotas(EXPERTS, rows)
-    named = jnp.logical_or(row == routes_t_ref[0:1, :], row == routes_t_ref[1:2, :])
+    named = jnp.logical_or(row == routes_ref[0:1, :], row == routes_ref[1:2, :])
     first, second = iotas(rows, rows)
     ranks = exact_dot(one_hot(named), one_hot(first < second))
     ranks = jnp.where(named, ranks, -1.0)
@@ -523,8 +450,7 @@
         arrived(squares.at[peer], sq_recv.at[peer])
     total = squares[0] + squares[1] + squares[2] + squares[3]
     inverse = lax.rsqrt(total / D + EPS)
-    inverse = jnp.broadcast_to(inverse[0:1, :], (rows, rows)).T[:, 0:1]
-    normed = (hidden[...] * inverse * gain_ref[...]).astype(jnp.bfloat16)
+    normed = (hidden[...] * upright(inverse[0:1, :]) * gain_ref[...]).astype(jnp.bfloat16)
     disp_m[...] = exact_dot(pick_main, normed).astype(jnp.bfloat16)
     overflow = exact_dot(pick_over, normed).astype(jnp.bfloat16)
     pieces = quarter // HD
@@ -640,8 +566,8 @@
 
         for n in range(hid_dev // HD):
             lanes = slice(n * HD, (n + 1) * HD)
-            gate = hid[0 : size + 16, lanes] * tall[n : n + 1, :]
-            up = hid[0 : size + 16, hid_dev + n * HD : hid_dev + (n + 1) * HD] * tall[n + 3 : n + 4, :]
+            gate = hid[0 : size + 16, lanes] * inner[0:1, lanes]
+            up = hid[0 : size + 16, hid_dev + n * HD : hid_dev + (n + 1) * HD] * inner[1:2, lanes]
             act[step * 272 : step * 272 + size + 16, lanes] = (
                 gate / (1.0 + jnp.exp(-gate)) * up
             ).astype(jnp.bfloat16)
@@ -690,12 +616,14 @@
                         sibling,
                     )
 
-    pump(3)
-    arrived(early_part, w_recv.at[4])
-    arrived(late_part, w_recv.at[5])
-    arrived(up_part, w_recv.at[0])
-    arrived(wide, w_recv.at[2])
-    arrived(tall, w_recv.at[3])
+    pump(2 * PIECES - progress[0])
+    for index in (0, 1, 4, 5):
+        arrived(moved[index][1], w_recv.at[index])
+    for line in range(4):
+        for n in range(pieces):
+            chunk = line * pieces + n
+            tall[line * 16 + n : line * 16 + n + 1, :] = wide[0:1, chunk * HD : (chunk + 1) * HD]
+        tall[line * 16 + pieces : (line + 1) * 16, :] = jnp.zeros((16 - pieces, HD), jnp.float32)
     for step in (0, 1, 2, 3):
         fetch_shared(step)
         hidden_part(step)
@@ -704,8 +632,8 @@
     share(major(4))
     fetch_shared(4)
     hidden_part(4)
-    pump(max(0, n_gate + PIECES + PIECES // 2 - progress[0]))
-    arrived(down_half[0], w_recv.at[1])
+    pump(2 * PIECES + PIECES // 2 - progress[0])
+    arrived(down_half[0], w_recv.at[2])
 
     def summed(own, others):
         value = own.astype(jnp.float32)
@@ -825,7 +753,7 @@
             value = tiles(OWN, last)
             for n in range(4):
                 eo_o[n * 64 : (n + 1) * 64, :] = (
-                    value[n * 64 : (n + 1) * 64, :] * tall[8:72, :]
+                    value[n * 64 : (n + 1) * 64, :] * tall[...]
                 ).astype(jnp.bfloat16)
         give_all(half, True)
         if half:
@@ -850,7 +778,7 @@
     hop_a(2, 0)
     hop_b(1, 0)
     pump(n_pieces)
-    arrived(down_half[1], w_recv.at[6])
+    arrived(down_half[1], w_recv.at[3])
     down_part(4, 1)
     hop_a(4, 1)
     down_part(3, 1)
@@ -868,7 +796,7 @@
     finish(1)
 
     expert_id = iotas(rows, EXPERTS)[1]
-    hits = [expert_id == routes_ref[:, k : k + 1] for k in range(2)]
+    hits = [expert_id == upright(routes_ref[k : k + 1, :]) for k in range(2)]
     first, second = iotas(rows, rows)
     both = one_hot(jnp.logical_or(hits[0], hits[1]))
     token_ranks = exact_dot(one_hot(second < first), both)
@@ -892,7 +820,7 @@
     routed = jnp.zeros((rows, quarter), jnp.float32)
     for k in range(2):
         picked = exact_dot(selects[k][0], ret_m[...]) + exact_dot(selects[k][1], back)
-        routed = routed + picked * weight_ref[:, k : k + 1]
+        routed = routed + picked * upright(weight_ref[k : k + 1, :])
     out_ref[...] = (hidden[...] + routed).astype(jnp.bfloat16)
 
     for copy in pending:
@@ -910,36 +838,34 @@
 
     @pl.when(swapping)
     def _():
-        for index in (2, 3):
+        for index in (4, 5):
             swap(index).wait_send()
         for number in range(n_pieces - IN_FLIGHT, n_pieces):
             load(number).wait_send()
 
 
-def experts(
-    residual, attended, norm_gain, routes, route_weight, gate_swapped, w_gate, w_up, w_down, scale_hidden, scale_out
+def layer(
+    queries, keys, values, residual, norm_gain, routes, route_weight, w_gate, w_up, w_down, scale_hidden, scale_out
 ):
     rows, quarter = residual.shape
-    width, hid_dev = w_gate.shape
-    wide = jnp.broadcast_to(scale_out, (8, width))
-    pieces = quarter // HD
-    tall = jnp.concatenate(
-        [
-            jnp.pad(scale_hidden.reshape(2 * hid_dev // HD, HD), ((0, 2), (0, 0))),
-            jnp.pad(scale_out.reshape(4, pieces, HD), ((0, 0), (0, 16 - pieces), (0, 0))).reshape(64, HD),
-        ],
-        axis=0,
-    )
+    _, width, hid_dev = w_gate.shape
+    length = rows * N_CTX
     vmem = pl.BlockSpec(memory_space=pltpu.VMEM)
     hbm = pl.BlockSpec(memory_space=pl.ANY)
     half = jnp.bfloat16
     dma = pltpu.SemaphoreType.DMA
     return pl.pallas_call(
-        expert_kernel,
+        layer_kernel,
         out_shape=jax.ShapeDtypeStruct((rows, quarter), half),
-        in_specs=[vmem] * 6 + [hbm] * 6,
+        in_specs=[vmem] * 3 + [hbm] * 9,
         out_specs=vmem,
         scratch_shapes=[
+            pltpu.VMEM((rows, quarter), half),
+            pltpu.VMEM((rows, quarter), half),
+            pltpu.VMEM((length, HD), half),
+            pltpu.VMEM((length, HD), half),
+            pltpu.VMEM((length, HD), half),
+            pltpu.VMEM((length, HD), half),
             pltpu.VMEM((16 * SLOT, width), half),
             pltpu.VMEM((16 * OVER, HD), half),
             pltpu.VMEM((16 * SLOT, width), half),
@@ -952,8 +878,9 @@
             pltpu.VMEM((3, OVER, HD), half),
             pltpu.VMEM((width, 2 * hid_dev), half),
             pltpu.VMEM((hid_dev, width), half),
-            pltpu.VMEM((8, width), jnp.float32),
-            pltpu.VMEM((72, HD), jnp.float32),
+            pltpu.VMEM((1, width), jnp.float32),
+            pltpu.VMEM((2, hid_dev), jnp.float32),
+            pltpu.VMEM((64, HD), jnp.float32),
             pltpu.VMEM((5 * 272, hid_dev), half),
             pltpu.VMEM((272, 2 * hid_dev), jnp.float32),
             pltpu.VMEM((rows, quarter), jnp.float32),
@@ -968,8 +895,8 @@
             pltpu.VMEM((36 * 16, 4 * OVER), half),
             pltpu.VMEM((4 * OVER, 36 * 16), half),
             pltpu.VMEM((4, 8, rows), jnp.float32),
-            dma((7,)),
-            dma((4,)),
+            dma((6,)),
+            dma((6,)),
             dma((4,)),
             dma((4,)),
             dma((2,)),
@@ -988,56 +915,31 @@
             dma((3, 3)),
             dma((2,)),
             dma((GROUP, 2)),
-            dma((3 * PIECES - EARLY,)),
+            dma((3 * PIECES,)),
+            dma((3,)),
+            dma((HEADS_HERE, 3)),
+            dma((N_CTX,)),
+            dma,
+            dma,
         ],
         compiler_params=pltpu.CompilerParams(
-            collective_id=1, has_side_effects=True, vmem_limit_bytes=60 * 1024 * 1024
+            collective_id=0, has_side_effects=True, vmem_limit_bytes=60 * 1024 * 1024
         ),
         cost_estimate=pl.CostEstimate(
-            flops=6 * 1088 * width * hid_dev, bytes_accessed=12 * 10**6, transcendentals=10**6
+            flops=6 * 1088 * width * hid_dev + 2 * length * length * HD, bytes_accessed=12 * 10**6, transcendentals=10**6
         ),
     )(
+        norm_gain.reshape(1, quarter),
+        routes.T,
+        route_weight.T,
         residual,
-        attended,
-        norm_gain.reshape(1, quarter),
-        routes,
-        routes.T,
-        route_weight,
+        queries,
+        keys,
+        values,
         w_gate,
-        gate_swapped,
         w_up,
         w_down,
-        wide,
-        tall,
-    )
-
-
-def local(
-    queries,
-    keys,
-    values,
-    residual,
-    norm_gain,
-    routes,
-    route_weight,
-    w_gate,
-    w_up,
-    w_down,
-    scale_hidden,
-    scale_out,
-):
-    attended, gate_swapped = attend(queries, keys, values, w_gate[0])
-    return experts(
-        residual,
-        attended,
-        norm_gain,
-        routes,
-        route_weight,
-        gate_swapped,
-        w_gate[0],
-        w_up[0],
-        w_down[0],
-        scale_hidden[0],
+        scale_hidden,
         scale_out,
     )
 
@@ -1058,4 +960,4 @@
         P(("dp", "tensor"), None),
     )
     out_specs = P(("dp", "context"), "tensor")
-    return jax.shard_map(local, mesh=mesh, in_specs=in_specs, out_specs=out_specs, check_vma=False)
+    return jax.shard_map(layer, mesh=mesh, in_specs=in_specs, out_specs=out_specs, check_vma=False)

time: 235 us -> 217 us (0.923); the launches traced: 232 us -> 217 us
  local copies, waits for them, and re-layouts: 12.5 us -> 2.99 us
  Pallas kernels: 218 us -> 214 us
    unnamed x13 -> x1, local copies, waits for them, and re-layouts: 9.86 us -> 1.7 us
    pallas_call x2 -> x1, Pallas kernels: 218 us -> 214 us  [layer(): pl.pallas_call(layer_kernel, out_shape=jax.ShapeDtypeStruct((rows, quarte...]
where the time goes in v4:
time: 217 us
  Pallas kernels  214 us (99%)
  local copies, waits for them, and re-layouts  2.99 us (1%)
    pallas_call x1, Pallas kernels, layer(): pl.pallas_call(layer_kernel, out_shape=jax.ShapeDtypeStruct((rows, quarte...  214 us

profile of v4, /device:TPU:8, one launch (start us, length us, event | category | flops | bytes accessed | tf_op | source)
XLA Modules:
  0.0 217.1 jit_solution(119852884378428797)
XLA Ops:
  0.0 1.3 reshape.3.gain_ref
  1.3 214.1 %shard_map.118 = bf16[128,1152]{1,0:T(8,128)(2,1)} custom-call(f32[1,1152]{1,0:T(1,128)} %reshape.3.gain_ref, s32[2,128]{1,0:T(2,128)} %bitcast.2, f32[2,128]{1,0:T(2,128)} %bitcast.3, bf16[128,1152]{1,0:T(8,128)(2,1)} %residual_ref.1, bf16[128,1152]{1,0:T(8,128)(2,1)} %q_ref.1, bf16[128,1152]{1,0:T(8,128)(2,1)} %k_ref.1, bf16[128,1152]{1,0:T(8,128)(2,1)} %v_ref.1, ...), custom_call_target="tpu_custom_call" | custom-call | flops 12624855040 | bytes 12000000 | tf_op jit(solution)/shard_map/pallas_call | solution.py:857
  215.4 1.7 copy.14

commit v5 on v4

--- a/solution.py
+++ b/solution.py
@@ -13,8 +13,8 @@
 EPS = 1e-06
 NEG = -1e30
 PIECES = 12
-IN_FLIGHT = 3
-EARLY = 12
+IN_FLIGHT = 5
+EARLY = 8
 N_CTX = 16
 HEADS_HERE = 9
 MESH = pl.DeviceIdType.MESH
@@ -26,7 +26,7 @@
 
 
 def attention_phase(
-    q_ref, k_ref, v_ref, out_ref, qs, ks, vs, ob, recv_sem, send_sem, out_send, out_recv, pump
+    q_ref, k_ref, v_ref, out_ref, qs, ks, vs, ob, recv_sem, send_sem, out_send, out_recv, pump, prepare
 ):
     ctx = lax.axis_index("context")
     core = lax.rem(lax.axis_index("dp"), 2)
@@ -69,6 +69,7 @@
         scatter(step, True)
 
     pump(0, 4)
+    prepare()
 
     base = lax.rem(ctx + 8 * core, N_CTX)
     my_head = lax.div(base * HEADS_HERE + N_CTX - 1, N_CTX)
@@ -236,7 +237,7 @@
     inner,
     tall,
     act,
-    hid,
+    gates,
     hidden,
     disp_m,
     disp_o,
@@ -246,6 +247,8 @@
     ret_o,
     over_x,
     over_y,
+    pick_m,
+    pick_o,
     spread,
     gather,
     squares,
@@ -406,8 +409,20 @@
         for index in range(6):
             pltpu.make_async_copy(moved[index][0], moved[index][1], w_recv.at[index]).start()
 
+    def prepare():
+        row, col = iotas(EXPERTS, rows)
+        named = jnp.logical_or(row == routes_ref[0:1, :], row == routes_ref[1:2, :])
+        first, second = iotas(rows, rows)
+        ranks = exact_dot(one_hot(named), one_hot(first < second))
+        ranks = jnp.where(named, ranks, -1.0)
+        row, col = iotas(EXPERTS * MAIN, EXPERTS)
+        widened = exact_dot(one_hot((row >> 4) == col), ranks.astype(jnp.bfloat16))
+        row, col = iotas(EXPERTS * MAIN, rows)
+        pick_m[...] = one_hot(widened == (row & 15).astype(jnp.float32))
+        pick_o[...] = one_hot(ranks == float(MAIN))
+
     attention_phase(
-        q_ref, k_ref, v_ref, attended, qs, ks, vs, ob, attn_recv, attn_send, out_send, out_recv, pump_at
+        q_ref, k_ref, v_ref, attended, qs, ks, vs, ob, attn_recv, attn_send, out_send, out_recv, pump_at, prepare
     )
     load_residual.wait()
 
@@ -434,25 +449,14 @@
         tell(step).start()
 
     pump(1)
-    row, col = iotas(EXPERTS, rows)
-    named = jnp.logical_or(row == routes_ref[0:1, :], row == routes_ref[1:2, :])
-    first, second = iotas(rows, rows)
-    ranks = exact_dot(one_hot(named), one_hot(first < second))
-    ranks = jnp.where(named, ranks, -1.0)
-    row, col = iotas(EXPERTS * MAIN, EXPERTS)
-    widened = exact_dot(one_hot((row >> 4) == col), ranks.astype(jnp.bfloat16))
-    row, col = iotas(EXPERTS * MAIN, rows)
-    pick_main = one_hot(widened == (row & 15).astype(jnp.float32))
-    pick_over = one_hot(ranks == float(MAIN))
-
     for step in (1, 2, 3):
         peer = lax.rem(tensor + step, 4)
         arrived(squares.at[peer], sq_recv.at[peer])
     total = squares[0] + squares[1] + squares[2] + squares[3]
     inverse = lax.rsqrt(total / D + EPS)
     normed = (hidden[...] * upright(inverse[0:1, :]) * gain_ref[...]).astype(jnp.bfloat16)
-    disp_m[...] = exact_dot(pick_main, normed).astype(jnp.bfloat16)
-    overflow = exact_dot(pick_over, normed).astype(jnp.bfloat16)
+    disp_m[...] = exact_dot(pick_m[...], normed).astype(jnp.bfloat16)
+    overflow = exact_dot(pick_o[...], normed).astype(jnp.bfloat16)
     pieces = quarter // HD
     stacked = jnp.concatenate(
         [overflow[:, n * HD : (n + 1) * HD] for n in range(pieces)], axis=0
@@ -531,16 +535,6 @@
     pass_on(OWN, major(1), aga_send, aga_recv, 0, ahead)
     pass_on(OWN, minor(1), agb_send, agb_recv, 0, behind)
     share(OWN)
-    for k in (1, 2, 3):
-        pump(4)
-        landed(major(k), aga_recv, k - 1)
-        pass_on(major(k), major(k + 1), aga_send, aga_recv, k, ahead)
-        share(major(k))
-        landed(minor(k), agb_recv, k - 1)
-        if k < 3:
-            pass_on(minor(k), minor(k + 1), agb_send, agb_recv, k, behind)
-        share(minor(k))
-
     def fetch_shared(step):
         low, count = STEPS[step]
         for slot in CARRIED:
@@ -550,27 +544,28 @@
     def step_rows(step):
         return STEPS[step][1] * SLOT
 
-    def hidden_part(step):
+    def rows_in(step):
+        low = STEPS[step][0] * SLOT
+        return jnp.concatenate(
+            [xm[low : low + step_rows(step), :], over_x[step * 16 : step * 16 + 16, :]], axis=0
+        )
+
+    def gate_products(step):
         low, count = STEPS[step]
-        size = step_rows(step)
+        size = step_rows(step) + 16
         tiles = xo[low * OVER : (low + count) * OVER, :]
         stack = exact_dot(spread[:, 0 : count * OVER], tiles).astype(jnp.bfloat16)
         for n in range(36):
-            over_x[:, n * HD : (n + 1) * HD] = stack[n * 16 : (n + 1) * 16, :]
-
-        @pl.loop(0, 3)
-        def _(n):
-            lanes = pl.ds(pl.multiple_of(n * 256, 256), 256)
-            rows_in = jnp.concatenate([xm[low * SLOT : low * SLOT + size, :], over_x[...]], axis=0)
-            hid[0 : size + 16, lanes] = exact_dot(rows_in, w1[:, lanes])
-
-        for n in range(hid_dev // HD):
-            lanes = slice(n * HD, (n + 1) * HD)
-            gate = hid[0 : size + 16, lanes] * inner[0:1, lanes]
-            up = hid[0 : size + 16, hid_dev + n * HD : hid_dev + (n + 1) * HD] * inner[1:2, lanes]
-            act[step * 272 : step * 272 + size + 16, lanes] = (
-                gate / (1.0 + jnp.exp(-gate)) * up
-            ).astype(jnp.bfloat16)
+            over_x[step * 16 : step * 16 + 16, n * HD : (n + 1) * HD] = stack[n * 16 : (n + 1) * 16, :]
+        gates[step * 272 : step * 272 + size, :] = exact_dot(rows_in(step), w1[:, 0:hid_dev])
+
+    def up_products(step):
+        size = step_rows(step) + 16
+        up = exact_dot(rows_in(step), w1[:, hid_dev : 2 * hid_dev]) * inner[1:2, :]
+        gate = gates[step * 272 : step * 272 + size, :] * inner[0:1, :]
+        act[step * 272 : step * 272 + size, :] = (gate / (1.0 + jnp.exp(-gate)) * up).astype(
+            jnp.bfloat16
+        )
 
     def lanes_of(half, n):
         start = half * half_width + n * 768
@@ -616,22 +611,39 @@
                         sibling,
                     )
 
+    for k in (1, 2, 3):
+        pump(6)
+        landed(major(k), aga_recv, k - 1)
+        pass_on(major(k), major(k + 1), aga_send, aga_recv, k, ahead)
+        share(major(k))
+        landed(minor(k), agb_recv, k - 1)
+        if k < 3:
+            pass_on(minor(k), minor(k + 1), agb_send, agb_recv, k, behind)
+        share(minor(k))
+        if k == 1:
+            arrived(gate_part, w_recv.at[0])
+        fetch_shared(k - 1)
+        gate_products(k - 1)
+    fetch_shared(3)
+    gate_products(3)
     pump(2 * PIECES - progress[0])
-    for index in (0, 1, 4, 5):
+    for index in (1, 4, 5):
         arrived(moved[index][1], w_recv.at[index])
     for line in range(4):
         for n in range(pieces):
             chunk = line * pieces + n
             tall[line * 16 + n : line * 16 + n + 1, :] = wide[0:1, chunk * HD : (chunk + 1) * HD]
         tall[line * 16 + pieces : (line + 1) * 16, :] = jnp.zeros((16 - pieces, HD), jnp.float32)
-    for step in (0, 1, 2, 3):
-        fetch_shared(step)
-        hidden_part(step)
+    for step in (0, 1, 2):
+        up_products(step)
         pump(1)
     landed(major(4), aga_recv, 3)
     share(major(4))
+    up_products(3)
+    pump(1)
     fetch_shared(4)
-    hidden_part(4)
+    gate_products(4)
+    up_products(4)
     pump(2 * PIECES + PIECES // 2 - progress[0])
     arrived(down_half[0], w_recv.at[2])
 
@@ -882,7 +894,7 @@
             pltpu.VMEM((2, hid_dev), jnp.float32),
             pltpu.VMEM((64, HD), jnp.float32),
             pltpu.VMEM((5 * 272, hid_dev), half),
-            pltpu.VMEM((272, 2 * hid_dev), jnp.float32),
+            pltpu.VMEM((5 * 272, hid_dev), jnp.float32),
             pltpu.VMEM((rows, quarter), jnp.float32),
             pltpu.VMEM((EXPERTS * MAIN, quarter), half),
             pltpu.VMEM((EXPERTS * TILE_ROWS, HD), half),
@@ -890,8 +902,10 @@
             pltpu.VMEM((OVER, HD), half),
             pltpu.VMEM((EXPERTS * MAIN, quarter), half),
             pltpu.VMEM((EXPERTS * TILE_ROWS, HD), half),
-            pltpu.VMEM((16, width), half),
             pltpu.VMEM((80, width), half),
+            pltpu.VMEM((80, width), half),
+            pltpu.VMEM((EXPERTS * MAIN, rows), half),
+            pltpu.VMEM((EXPERTS, rows), half),
             pltpu.VMEM((36 * 16, 4 * OVER), half),
             pltpu.VMEM((4 * OVER, 36 * 16), half),
             pltpu.VMEM((4, 8, rows), jnp.float32),

time: 217 us -> 207 us (0.954)
  Pallas kernels: 214 us -> 202 us
    pallas_call x1, Pallas kernels: 214 us -> 202 us  [layer(): pl.pallas_call(layer_kernel, out_shape=jax.ShapeDtypeStruct((rows, quarte...]
where the time goes in v5:
time: 207 us; the launch traced here: 205 us
  Pallas kernels  202 us (98%)
  local copies, waits for them, and re-layouts  2.99 us (1%)
    pallas_call x1, Pallas kernels, layer(): pl.pallas_call(layer_kernel, out_shape=jax.ShapeDtypeStruct((rows, quarte...  202 us

profile of v5, /device:TPU:8, one launch (start us, length us, event | category | flops | bytes accessed | tf_op | source)
XLA Modules:
  0.0 205.0 jit_solution(1363372988825421714)
XLA Ops:
  0.0 1.3 reshape.3.gain_ref
  1.3 202.0 %shard_map.118 = bf16[128,1152]{1,0:T(8,128)(2,1)} custom-call(f32[1,1152]{1,0:T(1,128)} %reshape.3.gain_ref, s32[2,128]{1,0:T(2,128)} %bitcast.2, f32[2,128]{1,0:T(2,128)} %bitcast.3, bf16[128,1152]{1,0:T(8,128)(2,1)} %residual_ref.1, bf16[128,1152]{1,0:T(8,128)(2,1)} %q_ref.1, bf16[128,1152]{1,0:T(8,128)(2,1)} %k_ref.1, bf16[128,1152]{1,0:T(8,128)(2,1)} %v_ref.1, ...), custom_call_target="tpu_custom_call" | custom-call | flops 12624855040 | bytes 12000000 | tf_op jit(solution)/shard_map/pallas_call | solution.py:869
  203.3 1.7 copy.14

commit v6 on v5

--- a/solution.py
+++ b/solution.py
@@ -823,6 +823,23 @@
     row, col = iotas(EXPERTS * pieces, EXPERTS * TILE_ROWS)
     unshuffle = one_hot((((row & 15) << 4) | (row >> 4)) == col)
 
+    for copy in pending:
+        copy.wait_send()
+    for step in (1, 2, 3):
+        tell(step).wait_send()
+
+    @pl.loop(1, GROUP)
+    def _(step):
+        for copy in dispatch(step):
+            copy.wait_send()
+
+    @pl.when(swapping)
+    def _():
+        for index in (4, 5):
+            swap(index).wait_send()
+        for number in range(n_pieces - IN_FLIGHT, n_pieces):
+            load(number).wait_send()
+
     arrived(ret_m, ret_recv.at[0])
     arrived(ret_o, ret_recv.at[1])
     back = exact_dot(unshuffle, ret_o[...]).astype(jnp.bfloat16)
@@ -835,25 +852,12 @@
         routed = routed + picked * upright(weight_ref[k : k + 1, :])
     out_ref[...] = (hidden[...] + routed).astype(jnp.bfloat16)
 
-    for copy in pending:
-        copy.wait_send()
-    for step in (1, 2, 3):
-        tell(step).wait_send()
+    for half in range(2):
+        give_all(half, False)
 
     @pl.loop(1, GROUP)
     def _(step):
-        for copy in dispatch(step) + [give_over(step)]:
-            copy.wait_send()
-
-    for half in range(2):
-        give_all(half, False)
-
-    @pl.when(swapping)
-    def _():
-        for index in (4, 5):
-            swap(index).wait_send()
-        for number in range(n_pieces - IN_FLIGHT, n_pieces):
-            load(number).wait_send()
+        give_over(step).wait_send()
 
 
 def layer(

time: 207 us -> 207 us (level)
  no operation moved by 1% of the time
where the time goes in v6:
time: 207 us; the launch traced here: 205 us
  Pallas kernels  202 us (98%)
  local copies, waits for them, and re-layouts  2.99 us (1%)
    pallas_call x1, Pallas kernels, layer(): pl.pallas_call(layer_kernel, out_shape=jax.ShapeDtypeStruct((rows, quarte...  202 us

profile of v6, /device:TPU:8, one launch (start us, length us, event | category | flops | bytes accessed | tf_op | source)
XLA Modules:
  0.0 204.8 jit_solution(282353847661608403)
XLA Ops:
  0.0 1.3 reshape.3.gain_ref
  1.3 201.8 %shard_map.118 = bf16[128,1152]{1,0:T(8,128)(2,1)} custom-call(f32[1,1152]{1,0:T(1,128)} %reshape.3.gain_ref, s32[2,128]{1,0:T(2,128)} %bitcast.2, f32[2,128]{1,0:T(2,128)} %bitcast.3, bf16[128,1152]{1,0:T(8,128)(2,1)} %residual_ref.1, bf16[128,1152]{1,0:T(8,128)(2,1)} %q_ref.1, bf16[128,1152]{1,0:T(8,128)(2,1)} %k_ref.1, bf16[128,1152]{1,0:T(8,128)(2,1)} %v_ref.1, ...), custom_call_target="tpu_custom_call" | custom-call | flops 12624855040 | bytes 12000000 | tf_op jit(solution)/shard_map/pallas_call | solution.py:873
  203.1 1.7 copy.14
